TPU v7x, 32 devices: a whole 2x2x4 slice. The times are simulated.
32 devices in a mesh: gx: 8 (over z, y), gz: 4 (over x, core).
Axes of the slice: x: 2, y: 2, z: 4, core: 2. Of those that a mesh axis runs over, the one named last changes fastest.
Arguments:
- solid_state: float32 [9, 20, 8192], P(None, None, ('gx', 'gz')), may hold values from -6 to 6
- jacobians: float32 [3, 9, 9, 8192], P(None, None, None, ('gx', 'gz')), may hold values from -2 to 2
- flux_solvers: float32 [4, 9, 9, 8192], P(None, None, None, ('gx', 'gz')), may hold values from -2 to 2
- stiffness: float32 [3, 20, 20], replicated, may hold values from -1.25 to 1.25
- trace_matrix: float32 [4, 10, 20], replicated, may hold values from -1.25 to 1.25
- lift_matrix: float32 [4, 20, 10], replicated, may hold values from -2 to 2
- neighbours: int32 [4, 8192], P(None, ('gx', 'gz')), may hold values from 0 to 1575, as said below
- send_faces: int32 [4, 4096], P(None, ('gx', 'gz')), may hold values from 0 to 1023, as said below
- surface_map: int32 [3, 5, 256], P(None, None, ('gx', 'gz')), may hold values from 0 to 16383, as said below
- surface_normals: float32 [3, 5, 256], P(None, None, ('gx', 'gz')), may hold values from -1 to 1
- air_state: float32 [4, 64, 64, 128], P(None, 'gx', 'gz'), may hold values from -6 to 6
- wind_field: float32 [3, 64, 64, 128], P(None, 'gx', 'gz'), may hold values from -0.3 to 0.3
- air_medium: float32 [2, 64, 64, 128], P(None, 'gx', 'gz'), may hold values from 0.05 to 0.25
Outputs:
- solid_next: float32 [9, 20, 8192], P(None, None, ('gx', 'gz'))
- air_next: float32 [4, 64, 64, 128], P(None, 'gx', 'gz')
Inputs may be any that keep to these rules, and one draw needn't show every extreme that they name: `neighbours`: entry [f, e] of a partition names what lies across face f of its tetrahedron e: below 1024 a face slot of the same partition (such slots name each other in pairs), from 1024 the slot 1024 + d * 128 + k of the k-th face shared in direction d, from 1536 the surface slot r * 8 + k. `send_faces`: the entries of a partition are distinct face slots; the face slot in [d, k] has neighbour entry 1024 + d * 128 + k. `surface_map`: row 0 holds distinct face slots, none of them in send_faces, whose neighbour entry is their surface slot; row 1 a cell index below 16384; row 2 is 1 for coupled slots and 0 otherwise. The coupled slots of one r are the lowest k; slots whose target strip lies outside 0 to 7 are uncoupled; the slots with r = 2 are all coupled.
All inputs are finite; a program needn't handle non-finite values.
Results may differ from a plain program's by a relative error of at most 0.0003.
Values sent between devices are 32-bit elements; how exact they have to be, the bound alone decides.
No kernel may reach another device: no remote copies, remote signals or barrier semaphores. Data moves between devices by JAX's collectives and lax.ppermute only.
A program may use at most 128 MiB of HBM per device.

v0:
```python
import functools

import jax
import jax.numpy as jnp
from jax import lax
from jax.experimental import pallas as pl
from jax.experimental.pallas import tpu as pltpu
from jax.sharding import PartitionSpec as P

ORDERS = 4
RADIUS = 4
SUBSTEPS = 3
ZRIM = 8
LANES = 128
TIME_STEP = 0.5
STENCIL_WEIGHTS = (0.8, -0.2, 4.0 / 105.0, -1.0 / 280.0)
F32 = jnp.float32
BF16 = jnp.bfloat16


def call(kernel, name, outs, ins, scratch=(), flops=1_000_000):
    nbytes = 4 * sum(x.size for x in ins) + 4 * sum(functools.reduce(lambda m, n: m * n, s, 1) for s in outs)
    return pl.pallas_call(
        kernel,
        out_shape=[jax.ShapeDtypeStruct(s, F32) for s in outs],
        in_specs=[pl.BlockSpec(memory_space=pltpu.VMEM) for _ in ins],
        out_specs=[pl.BlockSpec(memory_space=pltpu.VMEM) for _ in outs],
        scratch_shapes=[pltpu.VMEM(s, F32) for s in scratch],
        compiler_params=pltpu.CompilerParams(vmem_limit_bytes=24 * 1024 * 1024),
        cost_estimate=pl.CostEstimate(flops=flops, bytes_accessed=nbytes, transcendentals=0),
        name=name,
    )(*ins)


def swap(values, axis, odd):
    count = lax.axis_size(axis)
    pairs = []
    for i in range(odd, count - 1, 2):
        pairs += [(i, i + 1), (i + 1, i)]
    return lax.ppermute(values, axis, pairs)


def swap_pairs(values, odd):
    count = lax.axis_size("gx")
    pairs = []
    for i in range(count - 2):
        if i // 2 % 2 == odd:
            pairs += [(i, i + 2), (i + 2, i)]
    return lax.ppermute(values, "gx", pairs)


def exchange(xa, xb, za, zb):
    xb = swap(xb, "gx", 1)
    xa = swap(xa, "gx", 0)
    zb = swap(zb, "gz", 1)
    za = swap(za, "gz", 0)
    return za, zb, xa, xb


def sides(axis):
    parity = lax.axis_index(axis) & 1
    return 1 - parity, parity


def halves(values):
    high = values.astype(BF16)
    return high, (values - high.astype(F32)).astype(BF16)


def dot3(left, right, dims=(((1,), (0,)), ((), ()))):
    lh, ll = halves(left)
    rh, rl = halves(right)
    mul = functools.partial(lax.dot_general, dimension_numbers=dims, preferred_element_type=F32)
    return mul(lh, rh) + (mul(lh, rl) + mul(ll, rh))


def dot_exact(left, right, dims=(((1,), (0,)), ((), ()))):
    return lax.dot_general(
        left, right, dims, precision=lax.Precision.HIGHEST, preferred_element_type=F32
    )


def flat_slots(values):
    rows, slots = values.shape
    lane = lax.broadcasted_iota(jnp.int32, (slots, LANES), 1)
    place = lax.broadcasted_iota(jnp.int32, (slots, LANES), 0)
    spread = dot_exact(values, jnp.where(lane % slots == place, 1.0, 0.0).astype(F32))
    lane = lax.broadcasted_iota(jnp.int32, (rows, LANES), 1)
    place = lax.broadcasted_iota(jnp.int32, (rows, LANES), 0)
    return jnp.sum(jnp.where(lane // slots == place, spread, 0.0), axis=0, keepdims=True)


def pack_x(out, at, source, side):
    start = side * (source.shape[1] - RADIUS)
    out[pl.ds(at, source.shape[0])] = source[:, pl.ds(start, RADIUS)]


def pack_z(out, at, source, side):
    start = pl.multiple_of(side * (source.shape[2] - ZRIM), ZRIM)
    out[pl.ds(at, source.shape[0])] = source[:, :, pl.ds(start, ZRIM), :]


def widen(ext, center, za, zb, xa, xb, first=0, block=0):
    fields, nx, nz = center.shape[0], center.shape[1], center.shape[2]
    ext[:, RADIUS:RADIUS + nx, ZRIM:ZRIM + nz] = center[...]
    for got, side in zip((xa, xb), sides("gx")):
        place = pl.ds(side * (nx + RADIUS), RADIUS)
        if block:
            ext[0, place, ZRIM:ZRIM + nz] = got[(block - 1) * (1 - side)]
            ext[1:, place, ZRIM:ZRIM + nz] = got[block:block + fields - 1]
        else:
            skip = xa.shape[0] - za.shape[0] if first else 0
            ext[:, place, ZRIM:ZRIM + nz] = got[first + skip:first + skip + fields]
    for got, side in zip((za, zb), sides("gz")):
        start = pl.multiple_of(side * (nz + ZRIM), ZRIM)
        ext[:, RADIUS:RADIUS + nx, pl.ds(start, ZRIM)] = got[first:first + fields]


def d1(load, x, lo, hi):
    total = None
    for m, w in enumerate(STENCIL_WEIGHTS, 1):
        term = w * (load(x + m, lo, hi) - load(x - m, lo, hi))
        total = term if total is None else total + term
    return total


def d2(load, x, lo, hi):
    total = None
    for m, w in enumerate(STENCIL_WEIGHTS, 1):
        term = w * (load(x, lo + m, hi + m) - load(x, lo - m, hi - m))
        total = term if total is None else total + term
    return total


def d3(values):
    width = values.shape[1]
    lane = lax.broadcasted_iota(jnp.int32, (1, width), 1)
    total = None
    for m, w in enumerate(STENCIL_WEIGHTS, 1):
        ahead = jnp.where(lane < width - m, w, 0.0) * pltpu.roll(values, width - m, 1)
        behind = jnp.where(lane >= m, w, 0.0) * pltpu.roll(values, m, 1)
        term = ahead - behind
        total = term if total is None else total + term
    return total


def field(ref, c):
    return lambda x, lo, hi: ref[c, x, lo:hi, :]


def plane(ref):
    return lambda x, lo, hi: ref[x, lo:hi, :]


def arrived(table, strip, band, n_gx, n_gz, reach, slots):
    lane = lax.broadcasted_iota(jnp.int32, (1, LANES), 1)
    got = jnp.zeros((1, LANES), F32)
    inside = (strip >= 0) & (strip < n_gx) & (band >= 0) & (band < n_gz)
    for r in range(reach):
        source = strip - (r - reach // 2)
        valid = inside & (source >= 0) & (source < n_gx)
        at = jnp.where(valid, source * n_gz + band, 0)
        row = table[pl.ds(at, 1), :]
        scale = jnp.where(valid, 1.0, 0.0)
        got = jnp.where((lane & (LANES // 2 - 1)) // slots == r, row * scale, got)
    return got, pltpu.roll(got, LANES // 2, 1)


def cell_masks(cells, rows):
    cells = cells.astype(jnp.int32)
    place = lax.broadcasted_iota(jnp.int32, (rows, LANES), 0)
    third = lax.broadcasted_iota(jnp.int32, (LANES, LANES), 0)
    return cells // LANES == place, cells % LANES == third


def raw_rims_kernel(air, wind, xa, xb, za, zb, block):
    fields, nx = air.shape[:2]
    parts = nx // RADIUS
    block[...] = air[0]
    for out, side in zip((xa, xb), sides("gx")):
        start = side * (nx - RADIUS)
        for part in range(parts):
            out[part] = air[0, part * RADIUS:(part + 1) * RADIUS]
        out[parts:parts + fields - 1] = air[1:, pl.ds(start, RADIUS)]
        pack_x(out, parts + fields - 1, wind, side)
    for out, side in zip((za, zb), sides("gz")):
        pack_z(out, 0, air, side)
        pack_z(out, fields, wind, side)


def jacobian_step(jac, rot, emit):
    dims, quants = jac.shape[0], jac.shape[1]
    width = jac.shape[3]
    rows = rot.shape[0] // dims
    for h in range(width // LANES):
        at = h * LANES

        def body(d, acc):
            acc = list(acc)
            for q in range(quants):
                start = pl.multiple_of(d * rows, 8)
                turned = rot[pl.ds(start, rows), q * width + at:q * width + at + LANES]
                for p in range(quants):
                    acc[p] = acc[p] + jac[d, p, q:q + 1, at:at + LANES] * turned
            return tuple(acc)

        zeros = tuple(jnp.zeros((rows, LANES), F32) for _ in range(quants))
        acc = lax.fori_loop(0, dims, body, zeros)
        for p in range(quants):
            emit(p, at, acc[p])


def rotate(rot, matrix, source, quants, width):
    for q in range(quants):
        cut = slice(q * width, (q + 1) * width)
        rot[:, cut] = dot3(matrix[...], source[:, cut])


def take_slots(tiles, index):
    low = index % LANES
    high = index // LANES
    got = None
    for s, tile in enumerate(tiles):
        picked = jnp.take_along_axis(tile, low, axis=1, mode="promise_in_bounds")
        got = picked if got is None else jnp.where(high == s, picked, got)
    return got


def predict_kernel(
    state, jac, stiff, trace, sends, smap, normals,
    integral, traces, own, xa, xb, za, zb, rows,
    cur, rot, sp, tp, picked,
):
    quants, basis, width = state.shape
    pad = integral.shape[0]
    faces, face_basis = trace.shape[0], trace.shape[1]
    dims = stiff.shape[0]
    sp[...] = jnp.zeros_like(sp)
    tp[...] = jnp.zeros_like(tp)
    cur[...] = jnp.zeros_like(cur)
    for d in range(dims):
        sp[d * pad:d * pad + basis, 0:basis] = stiff[d]
    for f in range(faces):
        tp[f * 16:f * 16 + face_basis, 0:basis] = trace[f]
    for q in range(quants):
        cur[0:basis, q * width:(q + 1) * width] = state[q]
    integral[...] = TIME_STEP * cur[0:pad, :]

    def degree(k, weight):
        weight = jnp.where(k == 1, TIME_STEP**2 / 2, jnp.where(k == 2, TIME_STEP**3 / 6, TIME_STEP**4 / 24))
        rotate(rot, sp, cur, quants, width)

        def emit(p, at, value):
            cut = slice(p * width + at, p * width + at + LANES)
            cur[0:pad, cut] = -value
            integral[:, cut] = integral[:, cut] - weight * value

        jacobian_step(jac, rot, emit)
        return weight

    lax.fori_loop(1, ORDERS, degree, F32(0))
    for q in range(quants):
        cut = slice(q * width, (q + 1) * width)
        done = dot3(tp[:, 0:pad], integral[:, cut])
        for f in range(faces):
            traces[q, :, f * width:(f + 1) * width] = done[f * 16:(f + 1) * 16]
    slots = flat_slots(smap[0].astype(F32)).astype(jnp.int32)
    wanted = [jnp.broadcast_to(sends[d:d + 1, :], (16, LANES)) for d in range(4)]
    wanted.append(jnp.broadcast_to(slots, (16, LANES)))
    tiles_in = faces * width // LANES

    def gather(q, carry):
        tiles = [traces[q, :, s * LANES:(s + 1) * LANES] for s in range(tiles_in)]
        for d in range(4):
            picked[d, q] = take_slots(tiles, wanted[d])
        own[q] = take_slots(tiles, wanted[4])
        return carry

    lax.fori_loop(0, quants, gather, 0)
    for axis, base, outs in (("gx", 0, (xa, xb)), ("gz", 2, (za, zb))):
        for out, side in zip(outs, sides(axis)):
            for q in range(quants):
                out[q * 8:q * 8 + 8, :] = picked[base + side, q, 0:8, :]
                out[quants * 8 + q * 2:quants * 8 + q * 2 + 2, :] = picked[base + side, q, 8:face_basis, :]
            out[quants * face_basis:, :] = jnp.zeros((out.shape[0] - quants * face_basis, LANES), F32)
    coupled = flat_slots(smap[2].astype(F32))
    speed = jnp.zeros((1, LANES), F32)
    for c in range(3):
        mean = jnp.sum(own[6 + c, 0:face_basis, :], axis=0, keepdims=True) * (1.0 / face_basis)
        speed = speed + flat_slots(normals[c]) * mean
    lane = lax.broadcasted_iota(jnp.int32, (1, LANES), 1)
    cells = pltpu.roll(flat_slots(smap[1].astype(F32)), LANES // 2, 1)
    row = jnp.where(lane < LANES // 2, coupled * speed, cells)
    rows[...] = jnp.broadcast_to(row, rows.shape)


def pressure_rows(ext, wind, medium, x, nz):
    lo, hi = ZRIM, ZRIM + nz
    xe = x + RADIUS
    pressure = field(ext, 0)
    here = pressure(xe, lo, hi)
    divergence = d1(field(ext, 1), xe, lo, hi) + d2(field(ext, 2), xe, lo, hi) + d3(ext[3, xe, lo:hi, :])
    moved = (
        wind[0, x] * d1(pressure, xe, lo, hi)
        + wind[1, x] * d2(pressure, xe, lo, hi)
        + wind[2, x] * d3(here)
    )
    return here - medium[0, x] * divergence - moved


def pack_pressure(center, xa, xb, za, zb):
    nx, nz, ny = center.shape[1:]
    for out, side in zip((xa, xb), sides("gx")):
        start = side * (nx - RADIUS)
        out[0:RADIUS * nz, :] = center[0, pl.ds(start, RADIUS)].reshape(RADIUS * nz, ny)
    for out, side in zip((za, zb), sides("gz")):
        start = pl.multiple_of(side * (nz - ZRIM), ZRIM)
        out[0:nx * ZRIM, :] = center[0, :, pl.ds(start, ZRIM), :].reshape(nx * ZRIM, ny)


def widen_pressure(ext, center, za, zb, xa, xb):
    nx, nz, ny = center.shape
    ext[RADIUS:RADIUS + nx, ZRIM:ZRIM + nz] = center[...]
    for got, side in zip((xa, xb), sides("gx")):
        ext[pl.ds(side * (nx + RADIUS), RADIUS), ZRIM:ZRIM + nz] = got[0:RADIUS * nz, :].reshape(RADIUS, nz, ny)
    for got, side in zip((za, zb), sides("gz")):
        start = pl.multiple_of(side * (nz + ZRIM), ZRIM)
        ext[RADIUS:RADIUS + nx, pl.ds(start, ZRIM)] = got[0:nx * ZRIM, :].reshape(nx, ZRIM, ny)


def raw_pressure_kernel(
    air, wind, medium, za, zb, xa, xb, txa, txb, tza, tzb,
    pressure, oxa, oxb, oza, ozb, ext, fresh,
):
    nx, nz, ny = air.shape[1:]
    widen(ext, air, za, zb, xa, xb, block=nx // RADIUS)
    for x in range(nx):
        fresh[0, x] = pressure_rows(ext, wind, medium, x, nz)
    pressure[...] = fresh[0]
    pack_pressure(fresh, oxa, oxb, oza, ozb)
    for out, sent in zip((oxa, oxb, oza, ozb), (txa, txb, tza, tzb)):
        out[out.shape[0] - sent.shape[0]:, :] = sent[...]


def advection_kernel(block, air, wind, za, zb, xa, xb, moved, ext):
    nx, nz, ny = air.shape[1:]
    widen(ext, air, za, zb, xa, xb, block=block)
    lo, hi = ZRIM, ZRIM + nz
    for x in range(nx):
        xe = x + RADIUS
        for c in range(3):
            load = field(ext, 1 + c)
            moved[c, x] = (
                wind[0, x] * d1(load, xe, lo, hi)
                + wind[1, x] * d2(load, xe, lo, hi)
                + wind[2, x] * d3(load(xe, lo, hi))
            )


def velocities(out, center, moved, medium, wide, nx, nz):
    lo, hi = ZRIM, ZRIM + nz
    load = plane(wide)
    for x in range(nx):
        xe = x + RADIUS
        slopes = (d1(load, xe, lo, hi), d2(load, xe, lo, hi), d3(load(xe, lo, hi)))
        out[0, x] = load(xe, lo, hi)
        for c in range(3):
            out[1 + c, x] = center[1 + c, x] - medium[1, x] * slopes[c] - moved[c, x]


def pack_air(out, xa, xb, za, zb):
    for rim, side in zip((xa, xb), sides("gx")):
        pack_x(rim, 0, out, side)
    for rim, side in zip((za, zb), sides("gz")):
        pack_z(rim, 0, out, side)


def injected_kernel(
    n_gx, n_gz, air, wind, medium, raw, moved, wza, wzb, wxa, wxb, pza, pzb, pxa, pxb, lists, smap,
    out, oxa, oxb, oza, ozb, spread, wide, wide_wind,
):
    nx, nz, ny = air.shape[1:]
    reach, slots = smap.shape[1:]
    strip, band = lax.axis_index("gx"), lax.axis_index("gz")
    used = lax.broadcasted_iota(jnp.int32, (nx * nz, LANES), 1) < reach * slots
    for da in range(3):
        for db in range(3):
            where = (strip + da - 1, band + db - 1, n_gx, n_gz, reach, slots)
            speed, cells = arrived(lists, *where)
            row_mask, third_mask = cell_masks(cells, nx * nz)
            high, low = halves(jnp.where(row_mask & used, speed, 0.0))
            columns = jnp.where(third_mask, 1.0, 0.0).astype(BF16)
            mul = functools.partial(
                lax.dot_general, dimension_numbers=(((1,), (1,)), ((), ())), preferred_element_type=F32
            )
            block = mul(high, columns) + mul(low, columns)
            spread[da * nx:(da + 1) * nx, db * nz:(db + 1) * nz] = block.reshape(nx, nz, ny)
    widen(wide_wind, wind, wza, wzb, wxa, wxb, first=air.shape[0])
    widen_pressure(wide, raw, pza, pzb, pxa, pxb)
    load = plane(spread)
    for x in range(nx + 2 * RADIUS):
        xs = x + nx - RADIUS
        if RADIUS <= x < RADIUS + nx:
            lo, hi = 0, nz + 2 * ZRIM
        else:
            lo, hi = ZRIM, ZRIM + nz
        slo, shi = lo + nz - ZRIM, hi + nz - ZRIM
        here = load(xs, slo, shi)
        turned = (
            wide_wind[0, x, lo:hi, :] * d1(load, xs, slo, shi)
            + wide_wind[1, x, lo:hi, :] * d2(load, xs, slo, shi)
            + wide_wind[2, x, lo:hi, :] * d3(here)
        )
        wide[x, lo:hi, :] = wide[x, lo:hi, :] + (here - turned)
    velocities(out, air, moved, medium, wide, nx, nz)
    pack_air(out, oxa, oxb, oza, ozb)


def pressure_kernel(air, wind, medium, za, zb, xa, xb, pressure, oxa, oxb, oza, ozb, ext, fresh):
    nx, nz, ny = air.shape[1:]
    widen(ext, air, za, zb, xa, xb)
    for x in range(nx):
        fresh[0, x] = pressure_rows(ext, wind, medium, x, nz)
    pressure[...] = fresh[0]
    pack_pressure(fresh, oxa, oxb, oza, ozb)


def velocity_kernel(air, pressure, medium, moved, za, zb, xa, xb, out, *rest):
    nx, nz, ny = air.shape[1:]
    wide = rest[-1]
    widen_pressure(wide, pressure, za, zb, xa, xb)
    velocities(out, air, moved, medium, wide, nx, nz)
    if len(rest) > 1:
        pack_air(out, *rest[:-1])


def volume_kernel(state, integral, jac, stiff, out, rot, sp):
    quants, basis, width = state.shape
    pad = integral.shape[0]
    dims = stiff.shape[0]
    sp[...] = jnp.zeros_like(sp)
    place = lax.broadcasted_iota(jnp.int32, (basis, basis), 0)
    other = lax.broadcasted_iota(jnp.int32, (basis, basis), 1)
    unit = jnp.where(place == other, 1.0, 0.0).astype(F32)
    for d in range(dims):
        sp[d * pad:d * pad + basis, 0:basis] = dot_exact(unit, stiff[d], (((1,), (1,)), ((), ())))
    for q in range(quants):
        cut = slice(q * width, (q + 1) * width)
        rot[:, cut] = dot3(sp[:, 0:pad], integral[:, cut])

    def emit(p, at, value):
        out[p, :, at:at + LANES] = state[p, :, at:at + LANES] + value[0:basis]

    jacobian_step(jac, rot, emit)


def flux_kernel(
    n_gx, base, traces, own, solvers, lift, neighbours, smap, za, zb, xa, xb, air, nxa, nxb, fxa, fxb,
    out, tiles, flux, lp,
):
    quants, basis, width = base.shape
    faces, face_basis = lift.shape[0], lift.shape[2]
    reach, slots = smap.shape[1:]
    strip = lax.axis_index("gx")
    nx, nz, ny = air.shape[1:]
    rows = nx * nz
    lane = lax.broadcasted_iota(jnp.int32, (1, LANES), 1)
    cells = flat_slots(smap[1].astype(F32))
    row_mask, third_mask = cell_masks(cells, rows)
    columns = jnp.where(third_mask, 1.0, 0.0).astype(BF16)
    near, far = sides("gx")[0], 1 - (strip // 2) % 2
    near_blocks = [got[0:nx // RADIUS].reshape(rows, ny) for got in (nxa, nxb)]
    far_blocks = [got[...].reshape(rows, ny) for got in (fxa, fxb)]
    blocks = [
        jnp.where(far == 0, far_blocks[0], far_blocks[1]),
        jnp.where(near == 0, near_blocks[0], near_blocks[1]),
        air[0].reshape(rows, ny),
        jnp.where(near == 1, near_blocks[0], near_blocks[1]),
        jnp.where(far == 1, far_blocks[0], far_blocks[1]),
    ]
    replies = jnp.zeros((1, LANES), F32)
    for r in range(reach):
        high, low = halves(blocks[r])
        looked = jnp.dot(high, columns, preferred_element_type=F32)
        looked = looked + jnp.dot(low, columns, preferred_element_type=F32)
        found = jnp.sum(jnp.where(row_mask, looked, 0.0), axis=0, keepdims=True)
        replies = jnp.where(lane // slots == r, found, replies)
    replies = replies * flat_slots(smap[2].astype(F32))
    skip = xa.shape[0] - 96
    for axis, base_tile, gots in (("gx", 0, (xa, xb)), ("gz", 2, (za, zb))):
        for got, side in zip(gots, sides(axis)):
            for q in range(quants):
                tiles[q, base_tile + side, 0:8, :] = got[skip + q * 8:skip + q * 8 + 8, :]
                at = skip + quants * 8 + q * 2
                tiles[q, base_tile + side, 8:face_basis, :] = got[at:at + 2, :]
                tiles[q, base_tile + side, face_basis:, :] = jnp.zeros((16 - face_basis, LANES), F32)
    for q in range(quants):
        tiles[q, 4] = -2.0 * replies - own[q] if q < 3 else own[q]
    lp[...] = jnp.zeros_like(lp)
    for f in range(faces):
        lp[f, 0:basis, 0:face_basis] = lift[f]
    local = faces * width // LANES
    halves_in = width // LANES

    def one(t, carry):
        f = t // halves_in
        at = pl.multiple_of((t % halves_in) * LANES, LANES)
        index = neighbours[:, pl.ds(at, LANES)]
        face = lax.broadcasted_iota(jnp.int32, index.shape, 0)
        index = jnp.sum(jnp.where(face == f, index, 0), axis=0, keepdims=True)
        index = jnp.broadcast_to(index, (16, LANES))
        acc = [jnp.zeros((16, LANES), F32) for _ in range(quants)]
        for q in range(quants):
            pool = [traces[q, :, s * LANES:(s + 1) * LANES] for s in range(local)]
            pool += [tiles[q, s] for s in range(5)]
            mine = traces[q, :, pl.ds(pl.multiple_of(t * LANES, LANES), LANES)]
            jump = take_slots(pool, index) - mine
            for p in range(quants):
                acc[p] = acc[p] + solvers[f, p, q:q + 1, pl.ds(at, LANES)] * jump
        for p in range(quants):
            flux[f, :, pl.ds(pl.multiple_of(p * width + at, LANES), LANES)] = acc[p]
        return carry

    lax.fori_loop(0, local, one, 0)
    for p in range(quants):
        cut = slice(p * width, (p + 1) * width)
        total = base[p]
        for f in range(faces):
            total = total + dot3(lp[f, :, 0:16], flux[f, :, cut])[0:basis]
        out[p] = total


def shards(
    solid_state, jacobians, flux_solvers, stiffness, trace_matrix, lift_matrix,
    neighbours, send_faces, surface_map, surface_normals, air_state, wind_field, air_medium,
):
    quants, basis, width = solid_state.shape
    faces, face_basis = trace_matrix.shape[0], trace_matrix.shape[1]
    dims = stiffness.shape[0]
    nx, nz, ny = air_state.shape[1:]
    n_gx, n_gz = lax.axis_size("gx"), lax.axis_size("gz")
    devices = n_gx * n_gz
    pad = -(-basis // 8) * 8
    pad_k = -(-basis // 16) * 16
    parts = nx // RADIUS
    rim_x = (parts + 6, RADIUS, nz, ny)
    rim_z = (7, nx, ZRIM, ny)
    sent_rows = -(-quants * face_basis // 8) * 8
    ext = (4, nx + 2 * RADIUS, nz + 2 * ZRIM, ny)
    wide = ext[1:]

    xa, xb, za, zb, block = call(
        raw_rims_kernel, "raw_rims", [rim_x, rim_x, rim_z, rim_z, (nx, nz, ny)], [air_state, wind_field]
    )
    rims = exchange(xa, xb, za, zb)
    far = (swap_pairs(block, 0), swap_pairs(block, 1))

    sent = (sent_rows, LANES)
    integral, traces, own, txa, txb, tza, tzb, lists = call(
        predict_kernel, "predict",
        [(pad, quants * width), (quants, 16, faces * width), (quants, 16, LANES), sent, sent, sent, sent,
         (devices, LANES)],
        [solid_state, jacobians, stiffness, trace_matrix, send_faces, surface_map, surface_normals],
        [(pad_k, quants * width), (dims * pad, quants * width), (dims * pad, pad_k), (faces * 16, pad_k),
         (4, quants, 16, LANES)],
        flops=40_000_000,
    )
    both_x = (RADIUS * nz + sent_rows, LANES)
    both_z = (nx * ZRIM + sent_rows, LANES)
    raw, xa, xb, za, zb = call(
        raw_pressure_kernel, "raw_pressure",
        [(nx, nz, ny), both_x, both_x, both_z, both_z],
        [air_state, wind_field, air_medium, *rims, txa, txb, tza, tzb],
        [ext, (1, nx, nz, ny)],
    )
    both = exchange(xa, xb, za, zb)
    lists = lax.all_to_all(lists, ("gx", "gz"), split_axis=0, concat_axis=0, tiled=True)
    (moved,) = call(
        functools.partial(advection_kernel, parts), "advection", [(3, nx, nz, ny)],
        [air_state, wind_field, *rims], [ext], flops=10_000_000,
    )
    (volume,) = call(
        volume_kernel, "volume", [solid_state.shape], [solid_state, integral, jacobians, stiffness],
        [(dims * pad, quants * width), (dims * pad, pad_k)], flops=10_000_000,
    )

    raw_xa, raw_xb = rims[2:]
    rim_x = (4, RADIUS, nz, ny)
    rim_z = (4, nx, ZRIM, ny)
    air, xa, xb, za, zb = call(
        functools.partial(injected_kernel, n_gx, n_gz), "injected",
        [air_state.shape, rim_x, rim_x, rim_z, rim_z],
        [air_state, wind_field, air_medium, raw, moved, *rims, *both, lists, surface_map],
        [(3 * nx, 3 * nz, ny), wide, (3,) + wide],
    )
    for substep in range(1, SUBSTEPS):
        rims = exchange(xa, xb, za, zb)
        if substep == 1:
            (solid_next,) = call(
                functools.partial(flux_kernel, n_gx), "flux", [solid_state.shape],
                [volume, traces, own, flux_solvers, lift_matrix, neighbours, surface_map, *both,
                 air_state, raw_xa, raw_xb, *far],
                [(quants, 5, 16, LANES), (faces, 16, quants * width), (faces, pad, 16)], flops=20_000_000,
            )
        pressure, xa, xb, za, zb = call(
            pressure_kernel, "pressure",
            [(nx, nz, ny), (RADIUS * nz, ny), (RADIUS * nz, ny), (nx * ZRIM, ny), (nx * ZRIM, ny)],
            [air, wind_field, air_medium, *rims], [ext, (1, nx, nz, ny)],
        )
        rises = exchange(xa, xb, za, zb)
        (moved,) = call(
            functools.partial(advection_kernel, 0), "advection", [(3, nx, nz, ny)],
            [air, wind_field, *rims], [ext], flops=10_000_000,
        )
        last = substep == SUBSTEPS - 1
        outs = [air_state.shape] + ([] if last else [rim_x, rim_x, rim_z, rim_z])
        done = call(
            velocity_kernel, "velocity", outs, [air, pressure, air_medium, moved, *rises], [wide]
        )
        air = done[0]
        if not last:
            xa, xb, za, zb = done[1:]
    return (solid_next, air)


def solution(mesh):
    in_specs = (
        P(None, None, ("gx", "gz")),
        P(None, None, None, ("gx", "gz")),
        P(None, None, None, ("gx", "gz")),
        P(),
        P(),
        P(),
        P(None, ("gx", "gz")),
        P(None, ("gx", "gz")),
        P(None, None, ("gx", "gz")),
        P(None, None, ("gx", "gz")),
        P(None, "gx", "gz", None),
        P(None, "gx", "gz", None),
        P(None, "gx", "gz", None),
    )
    out_specs = (P(None, None, ("gx", "gz")), P(None, "gx", "gz", None))
    return jax.shard_map(shards, mesh=mesh, in_specs=in_specs, out_specs=out_specs, check_vma=False)
```

profile of v0, /device:TPU:5, one launch (start us, length us, event | category | flops | bytes accessed | tf_op | source)
XLA Modules:
  0.0 95.1 jit_solution(8177156622372835992)
XLA Ops:
  0.6 0.9 copy-done
  1.6 0.9 copy-done.2
  3.2 4.4 %collective-permute-start.3 = (f32[8,4,16,128]{3,2,1,0:T(8,128)S(1)}, f32[8,4,16,128]{3,2,1,0:T(8,128)S(1)}, u32[]{:S(2)}, u32[]{:S(2)}) collective-permute-start(f32[8,4,16,128]{3,2,1,0:T(8,128)S(1)} %get-tuple-element.46), channel_id=1, source_target_pairs={{4,8},{8,4},{12,16},{16,12},{20,24},{24,20},{5,9},{9,5},{13,17},{1... | collective-permute-start | bytes 786440 | tf_op jit(solution)/shard_map/ppermute | solution.py:40
  7.6 1.3 %collective-permute-start = (f32[7,8,8,128]{3,2,1,0:T(8,128)S(1)}, f32[7,8,8,128]{3,2,1,0:T(8,128)S(1)}, u32[]{:S(2)}, u32[]{:S(2)}) collective-permute-start(f32[7,8,8,128]{3,2,1,0:T(8,128)S(1)} %get-tuple-element.43), channel_id=1, source_target_pairs={{0,1},{1,0},{2,3},{3,2},{4,5},{5,4},{6,7},{7,6},{8,9},{9,8},{10,11... | collective-permute-start | bytes 688136 | tf_op jit(solution)/shard_map/ppermute | solution.py:40
  8.9 3.0 %collective-permute-start.1 = (f32[7,8,8,128]{3,2,1,0:T(8,128)S(1)}, f32[7,8,8,128]{3,2,1,0:T(8,128)S(1)}, u32[]{:S(2)}, u32[]{:S(2)}) collective-permute-start(f32[7,8,8,128]{3,2,1,0:T(8,128)S(1)} %get-tuple-element.44), channel_id=1, source_target_pairs={{1,2},{2,1},{5,6},{6,5},{9,10},{10,9},{13,14},{14,13},{17,18},{18,... | collective-permute-start | bytes 688136 | tf_op jit(solution)/shard_map/ppermute | solution.py:40
  14.2 5.7 %predict.1 = (f32[24,2304]{1,0:T(8,128)S(1)}, f32[9,16,1024]{2,1,0:T(8,128)S(1)}, f32[9,16,128]{2,1,0:T(8,128)S(1)}, f32[96,128]{1,0:T(8,128)S(1)}, f32[96,128]{...) custom-call(f32[9,20,256]{2,1,0:T(8,128)S(1)} %copy-done.5, ...), custom_call_target="tpu_custom_call" | custom-call | flops 40000000 | bytes 1541888 | tf_op jit(solution)/shard_map/predict/pallas_call | solution.py:23
  19.9 1.1 %raw_pressure.1 = (f32[8,16,128]{2,1,0:T(8,128)S(1)}, f32[160,128]{1,0:T(8,128)}, f32[160,128]{1,0:T(8,128)}, f32[160,128]{1,0:T(8,128)}, f32[160,128]{1,0:T(8,128)}) custom-call(f32[4,8,16,128]{3,2,1,0:T(8,128)S(1)} %copy-done.3, f32[3,8,16,128]{3,2,1,0:T(8,128)S(1)} %copy-done.1, f32[2,8,16,128]{3,2,1,0:T(8,128)S(1)} %copy-done.4, ...), custom_call_target="tpu_custom_call" | custom-call | flops 1000000 | bytes 2162688 | tf_op jit(solution)/shard_map/raw_pressure/pallas_call | solution.py:23
  21.1 2.6 %collective-permute-start.5 = (f32[160,128]{1,0:T(8,128)}, f32[160,128]{1,0:T(8,128)S(1)}, u32[]{:S(2)}, u32[]{:S(2)}) collective-permute-start(f32[160,128]{1,0:T(8,128)} %get-tuple-element.52), channel_id=1, source_target_pairs={{1,2},{2,1},{5,6},{6,5},{9,10},{10,9},{13,14},{14,13},{17,18},{18,... | collective-permute-start | bytes 245768 | tf_op jit(solution)/shard_map/ppermute | solution.py:40
  23.9 4.4 %collective-permute-start.7 = (f32[160,128]{1,0:T(8,128)}, f32[160,128]{1,0:T(8,128)S(1)}, u32[]{:S(2)}, u32[]{:S(2)}) collective-permute-start(f32[160,128]{1,0:T(8,128)} %get-tuple-element.54), channel_id=1, source_target_pairs={{4,8},{8,4},{12,16},{16,12},{20,24},{24,20},{5,9},{9,5},{13,17},{1... | collective-permute-start | bytes 245768 | tf_op jit(solution)/shard_map/ppermute | solution.py:40
  28.2 4.2 %all-to-all-start = ((f32[32,1,128]{2,1,0:T(1,128)}), f32[32,1,128]{2,1,0:T(1,128)S(1)}, u32[]{:S(2)}, u32[]{:S(2)}) async-start(f32[32,1,128]{2,1,0:T(1,128)} %bitcast.1), calls=%async_computation | async-start | bytes 32768 | tf_op jit(solution)/shard_map/all_to_all | solution.py:577
  32.9 5.1 %all-to-all-done = f32[32,1,128]{2,1,0:T(1,128)S(1)} async-done(((f32[32,1,128]{2,1,0:T(1,128)}), f32[32,1,128]{2,1,0:T(1,128)S(1)}, u32[]{:S(2)}, u32[]{:S(2)}) %all-to-all-start) | async-done | bytes 16416 | tf_op jit(solution)/shard_map/all_to_all | solution.py:577
  38.1 1.2 %injected.1 = (f32[4,8,16,128]{3,2,1,0:T(8,128)S(1)}, f32[4,4,16,128]{3,2,1,0:T(8,128)S(1)}, f32[4,4,16,128]{3,2,1,0:T(8,128)S(1)}, f32[4,8,8,128]{3,2,1,0:T(8,128)S(1)}, f32[4,8,8,128]{3,2,1,0:T(8,128)S(1)}) custom-call(f32[4,8,16,128]{3,2,1,0:T(8,128)S(1)} %copy-done.3, f32[3,8,16,128]{3,2,1,0:T(8,128)S(1)} %copy-done.1, f32[2,8,16,128]{3,2,1,0:T(8,128)S(1)} %copy-done.4, ...), custom_call_target="tpu_custom_call" | custom-call | flops 1000000 | bytes 2965984 | tf_op jit(solution)/shard_map/injected/pallas_call | solution.py:23
  40.0 2.2 %collective-permute-start.11 = (f32[4,8,8,128]{3,2,1,0:T(8,128)S(1)}, f32[4,8,8,128]{3,2,1,0:T(8,128)S(1)}, u32[]{:S(2)}, u32[]{:S(2)}) collective-permute-start(f32[4,8,8,128]{3,2,1,0:T(8,128)S(1)} %get-tuple-element.60), channel_id=1, source_target_pairs={{1,2},{2,1},{5,6},{6,5},{9,10},{10,9},{13,14},{14,13},{17,18},{18,... | collective-permute-start | bytes 393224 | tf_op jit(solution)/shard_map/ppermute | solution.py:40
  42.2 1.2 %collective-permute-start.12 = (f32[4,4,16,128]{3,2,1,0:T(8,128)S(1)}, f32[4,4,16,128]{3,2,1,0:T(8,128)S(1)}, u32[]{:S(2)}, u32[]{:S(2)}) collective-permute-start(f32[4,4,16,128]{3,2,1,0:T(8,128)S(1)} %get-tuple-element.61), channel_id=1, source_target_pairs={{0,4},{4,0},{8,12},{12,8},{16,20},{20,16},{24,28},{28,24},{1,5},{5... | collective-permute-start | bytes 393224 | tf_op jit(solution)/shard_map/ppermute | solution.py:40
  43.4 2.3 %collective-permute-start.13 = (f32[4,4,16,128]{3,2,1,0:T(8,128)S(1)}, f32[4,4,16,128]{3,2,1,0:T(8,128)S(1)}, u32[]{:S(2)}, u32[]{:S(2)}) collective-permute-start(f32[4,4,16,128]{3,2,1,0:T(8,128)S(1)} %get-tuple-element.62), channel_id=1, source_target_pairs={{4,8},{8,4},{12,16},{16,12},{20,24},{24,20},{5,9},{9,5},{13,17},{1... | collective-permute-start | bytes 393224 | tf_op jit(solution)/shard_map/ppermute | solution.py:40
  46.5 4.3 %collective-permute-done.13.xb = f32[4,4,16,128]{3,2,1,0:T(8,128)S(1)} collective-permute-done((f32[4,4,16,128]{3,2,1,0:T(8,128)S(1)}, f32[4,4,16,128]{3,2,1,0:T(8,128)S(1)}, u32[]{:S(2)}, u32[]{:S(2)}) %collective-permute-start.13) | collective-permute-done | bytes 131104 | tf_op jit(solution)/shard_map/ppermute | solution.py:40
  51.3 4.1 %collective-permute-start.15 = (f32[64,128]{1,0:T(8,128)S(1)}, f32[64,128]{1,0:T(8,128)S(1)}, u32[]{:S(2)}, u32[]{:S(2)}) collective-permute-start(f32[64,128]{1,0:T(8,128)S(1)} %get-tuple-element.65), channel_id=1, source_target_pairs={{1,2},{2,1},{5,6},{6,5},{9,10},{10,9},{13,14},{14,13},{17,18},{18,... | collective-permute-start | bytes 98312 | tf_op jit(solution)/shard_map/ppermute | solution.py:40
  55.4 3.4 %collective-permute-start.17 = (f32[64,128]{1,0:T(8,128)S(1)}, f32[64,128]{1,0:T(8,128)S(1)}, u32[]{:S(2)}, u32[]{:S(2)}) collective-permute-start(f32[64,128]{1,0:T(8,128)S(1)} %get-tuple-element.67), channel_id=1, source_target_pairs={{4,8},{8,4},{12,16},{16,12},{20,24},{24,20},{5,9},{9,5},{13,17},{1... | collective-permute-start | bytes 98312 | tf_op jit(solution)/shard_map/ppermute | solution.py:40
  59.3 1.7 %collective-permute-done.17.xb = f32[64,128]{1,0:T(8,128)S(1)} collective-permute-done((f32[64,128]{1,0:T(8,128)S(1)}, f32[64,128]{1,0:T(8,128)S(1)}, u32[]{:S(2)}, u32[]{:S(2)}) %collective-permute-start.17) | collective-permute-done | bytes 32800 | tf_op jit(solution)/shard_map/ppermute | solution.py:40
  61.4 3.1 %collective-permute-start.19 = (f32[4,8,8,128]{3,2,1,0:T(8,128)S(1)}, f32[4,8,8,128]{3,2,1,0:T(8,128)S(1)}, u32[]{:S(2)}, u32[]{:S(2)}) collective-permute-start(f32[4,8,8,128]{3,2,1,0:T(8,128)S(1)} %get-tuple-element.70), channel_id=1, source_target_pairs={{1,2},{2,1},{5,6},{6,5},{9,10},{10,9},{13,14},{14,13},{17,18},{18,... | collective-permute-start | bytes 393224 | tf_op jit(solution)/shard_map/ppermute | solution.py:40
  64.5 3.9 %collective-permute-start.21 = (f32[4,4,16,128]{3,2,1,0:T(8,128)S(1)}, f32[4,4,16,128]{3,2,1,0:T(8,128)S(1)}, u32[]{:S(2)}, u32[]{:S(2)}) collective-permute-start(f32[4,4,16,128]{3,2,1,0:T(8,128)S(1)} %get-tuple-element.72), channel_id=1, source_target_pairs={{4,8},{8,4},{12,16},{16,12},{20,24},{24,20},{5,9},{9,5},{13,17},{1... | collective-permute-start | bytes 393224 | tf_op jit(solution)/shard_map/ppermute | solution.py:40
  68.8 1.3 %collective-permute-start.9 = (f32[8,16,128]{2,1,0:T(8,128)}, f32[8,16,128]{2,1,0:T(8,128)}, u32[]{:S(2)}, u32[]{:S(2)}) collective-permute-start(f32[8,16,128]{2,1,0:T(8,128)} %get-tuple-element.55), channel_id=1, source_target_pairs={{8,16},{16,8},{12,20},{20,12},{9,17},{17,9},{13,21},{21,13},{10,18... | collective-permute-start | bytes 196616 | tf_op jit(solution)/shard_map/ppermute | solution.py:49
  70.1 1.7 %collective-permute-done.21.xb = f32[4,4,16,128]{3,2,1,0:T(8,128)S(1)} collective-permute-done((f32[4,4,16,128]{3,2,1,0:T(8,128)S(1)}, f32[4,4,16,128]{3,2,1,0:T(8,128)S(1)}, u32[]{:S(2)}, u32[]{:S(2)}) %collective-permute-start.21) | collective-permute-done | bytes 131104 | tf_op jit(solution)/shard_map/ppermute | solution.py:40
  71.8 1.1 %pressure.3 = (f32[8,16,128]{2,1,0:T(8,128)S(1)}, f32[64,128]{1,0:T(8,128)}, f32[64,128]{1,0:T(8,128)}, f32[64,128]{1,0:T(8,128)}, f32[64,128]{1,0:T(8,128)}) custom-call(f32[4,8,16,128]{3,2,1,0:T(8,128)S(1)} %get-tuple-element.68.air, f32[3,8,16,128]{3,2,1,0:T(8,128)S(1)} %copy-done.1, f32[2,8,16,128]{3,2,1,0:T(8,128)S(1)} %copy-done.4, ...), custom_call_target="tpu_custom_call" | custom-call | flops 1000000 | bytes 1310720 | tf_op jit(solution)/shard_map/pressure/pallas_call | solution.py:23
  73.5 3.0 %collective-permute-start.23 = (f32[64,128]{1,0:T(8,128)}, f32[64,128]{1,0:T(8,128)}, u32[]{:S(2)}, u32[]{:S(2)}) collective-permute-start(f32[64,128]{1,0:T(8,128)} %get-tuple-element.75), channel_id=1, source_target_pairs={{1,2},{2,1},{5,6},{6,5},{9,10},{10,9},{13,14},{14,13},{17,18},{18,... | collective-permute-start | bytes 98312 | tf_op jit(solution)/shard_map/ppermute | solution.py:40
  77.2 5.8 %collective-permute-start.25 = (f32[64,128]{1,0:T(8,128)}, f32[64,128]{1,0:T(8,128)}, u32[]{:S(2)}, u32[]{:S(2)}) collective-permute-start(f32[64,128]{1,0:T(8,128)} %get-tuple-element.77), channel_id=1, source_target_pairs={{4,8},{8,4},{12,16},{16,12},{20,24},{24,20},{5,9},{9,5},{13,17},{1... | collective-permute-start | bytes 98312 | tf_op jit(solution)/shard_map/ppermute | solution.py:40
  83.1 0.8 copy.30.lift
  83.9 0.9 copy-done.19
  84.9 0.8 copy-done.21
  85.7 1.1 %volume.1.base = f32[9,20,256]{2,1,0:T(8,128)S(1)} custom-call(f32[9,20,256]{2,1,0:T(8,128)S(1)} %copy-done.5, f32[24,2304]{1,0:T(8,128)S(1)} %copy-done.19, f32[3,9,9,256]{3,2,1,0:T(8,128)S(1)} %copy.24.jac, f32[3,20,20]{2,1,0:T(8,128)S(1)} %copy-done.21), custom_call_target="tpu_custom_call" | custom-call | flops 10000000 | bytes 843456 | tf_op jit(solution)/shard_map/volume/pallas_call | solution.py:23
  86.9 5.5 %flux.1 = f32[9,20,256]{2,1,0:T(8,128)} custom-call(f32[9,20,256]{2,1,0:T(8,128)S(1)} %volume.1.base, f32[9,16,1024]{2,1,0:T(8,128)S(1)} %get-tuple-element.41.traces, f32[9,16,128]{2,1,0:T(8,128)S(1)} %copy-done.23, f32[4,9,9,256]{3,2,1,0:T(8,128)S(1)} %copy.29.solvers, f32[4,20,10]{2,1,0:T(8,128)S(1)} %copy.30.lift, s32[4,256]{1,0:T(4,128)S(1)} %copy-done.28, ...), custom_call_target="tpu_custom_call" | custom-call | flops 20000000 | bytes 2616928 | tf_op jit(solution)/shard_map/flux/pallas_call | solution.py:23
  93.3 1.8 %velocity.3 = f32[4,8,16,128]{3,2,1,0:T(8,128)} custom-call(f32[4,8,16,128]{3,2,1,0:T(8,128)S(1)} %get-tuple-element.68.air, f32[8,16,128]{2,1,0:T(8,128)S(1)} %copy-done.25, f32[2,8,16,128]{3,2,1,0:T(8,128)S(1)} %copy-done.4, f32[3,8,16,128]{3,2,1,0:T(8,128)S(1)} %advection.5.moved, f32[64,128]{1,0:T(8,128)} %collective-permute-done.22.za, ...), custom_call_target="tpu_custom_call" | custom-call | flops 1000000 | bytes 1048576 | tf_op jit(solution)/shard_map/velocity/pallas_call | solution.py:23
  (111 shorter events, 9.3 us)
Async XLA Ops:
  2.5 9.4 %copy-start.31 = (f32[3,9,9,256]{3,0,2,1:T(4,128)S(1)}, f32[3,9,9,256]{3,0,2,1:T(4,128)}, u32[]{:S(2)}) copy-start(f32[3,9,9,256]{3,0,2,1:T(4,128)} %param.14) | copy-start | bytes 746500
  3.2 16.7 %collective-permute-start.2 = (f32[8,4,16,128]{3,2,1,0:T(8,128)S(1)}, f32[8,4,16,128]{3,2,1,0:T(8,128)S(1)}, u32[]{:S(2)}, u32[]{:S(2)}) collective-permute-start(f32[8,4,16,128]{3,2,1,0:T(8,128)S(1)} %get-tuple-element.45), channel_id=1, source_target_pairs={{0,4},{4,0},{8,12},{12,8},{16,20},{20,16},{24,28},{28,24},{1,5},{5... | collective-permute-start | bytes 786440 | tf_op jit(solution)/shard_map/ppermute | solution.py:40
  3.2 16.7 %collective-permute-start.3 = (f32[8,4,16,128]{3,2,1,0:T(8,128)S(1)}, f32[8,4,16,128]{3,2,1,0:T(8,128)S(1)}, u32[]{:S(2)}, u32[]{:S(2)}) collective-permute-start(f32[8,4,16,128]{3,2,1,0:T(8,128)S(1)} %get-tuple-element.46), channel_id=1, source_target_pairs={{4,8},{8,4},{12,16},{16,12},{20,24},{24,20},{5,9},{9,5},{13,17},{1... | collective-permute-start | bytes 786440 | tf_op jit(solution)/shard_map/ppermute | solution.py:40
  7.6 12.3 %collective-permute-start = (f32[7,8,8,128]{3,2,1,0:T(8,128)S(1)}, f32[7,8,8,128]{3,2,1,0:T(8,128)S(1)}, u32[]{:S(2)}, u32[]{:S(2)}) collective-permute-start(f32[7,8,8,128]{3,2,1,0:T(8,128)S(1)} %get-tuple-element.43), channel_id=1, source_target_pairs={{0,1},{1,0},{2,3},{3,2},{4,5},{5,4},{6,7},{7,6},{8,9},{9,8},{10,11... | collective-permute-start | bytes 688136 | tf_op jit(solution)/shard_map/ppermute | solution.py:40
  8.9 11.0 %collective-permute-start.1 = (f32[7,8,8,128]{3,2,1,0:T(8,128)S(1)}, f32[7,8,8,128]{3,2,1,0:T(8,128)S(1)}, u32[]{:S(2)}, u32[]{:S(2)}) collective-permute-start(f32[7,8,8,128]{3,2,1,0:T(8,128)S(1)} %get-tuple-element.44), channel_id=1, source_target_pairs={{1,2},{2,1},{5,6},{6,5},{9,10},{10,9},{13,14},{14,13},{17,18},{18,... | collective-permute-start | bytes 688136 | tf_op jit(solution)/shard_map/ppermute | solution.py:40
  14.2 5.7 %copy-start.1 = (f32[3,8,16,128]{3,2,1,0:T(8,128)S(1)}, f32[3,8,16,128]{3,2,1,0:T(8,128)}, u32[]{:S(2)}) copy-start(f32[3,8,16,128]{3,2,1,0:T(8,128)} %wind.15) | copy-start | bytes 589828
  14.2 5.7 %copy-start.3 = (f32[4,8,16,128]{3,2,1,0:T(8,128)S(1)}, f32[4,8,16,128]{3,2,1,0:T(8,128)}, u32[]{:S(2)}) copy-start(f32[4,8,16,128]{3,2,1,0:T(8,128)} %air.9) | copy-start | bytes 786436
  14.2 5.8 %copy-start.4 = (f32[2,8,16,128]{3,2,1,0:T(8,128)S(1)}, f32[2,8,16,128]{3,2,1,0:T(8,128)}, u32[]{:S(2)}) copy-start(f32[2,8,16,128]{3,2,1,0:T(8,128)} %medium.11) | copy-start | bytes 393220
  21.1 17.0 %collective-permute-start.4 = (f32[160,128]{1,0:T(8,128)}, f32[160,128]{1,0:T(8,128)S(1)}, u32[]{:S(2)}, u32[]{:S(2)}) collective-permute-start(f32[160,128]{1,0:T(8,128)} %get-tuple-element.51), channel_id=1, source_target_pairs={{0,1},{1,0},{2,3},{3,2},{4,5},{5,4},{6,7},{7,6},{8,9},{9,8},{10,11... | collective-permute-start | bytes 245768 | tf_op jit(solution)/shard_map/ppermute | solution.py:40
  21.1 16.9 %collective-permute-start.5 = (f32[160,128]{1,0:T(8,128)}, f32[160,128]{1,0:T(8,128)S(1)}, u32[]{:S(2)}, u32[]{:S(2)}) collective-permute-start(f32[160,128]{1,0:T(8,128)} %get-tuple-element.52), channel_id=1, source_target_pairs={{1,2},{2,1},{5,6},{6,5},{9,10},{10,9},{13,14},{14,13},{17,18},{18,... | collective-permute-start | bytes 245768 | tf_op jit(solution)/shard_map/ppermute | solution.py:40
  23.8 14.3 %collective-permute-start.6 = (f32[160,128]{1,0:T(8,128)}, f32[160,128]{1,0:T(8,128)S(1)}, u32[]{:S(2)}, u32[]{:S(2)}) collective-permute-start(f32[160,128]{1,0:T(8,128)} %get-tuple-element.53), channel_id=1, source_target_pairs={{0,4},{4,0},{8,12},{12,8},{16,20},{20,16},{24,28},{28,24},{1,5},{5... | collective-permute-start | bytes 245768 | tf_op jit(solution)/shard_map/ppermute | solution.py:40
  23.9 14.2 %collective-permute-start.7 = (f32[160,128]{1,0:T(8,128)}, f32[160,128]{1,0:T(8,128)S(1)}, u32[]{:S(2)}, u32[]{:S(2)}) collective-permute-start(f32[160,128]{1,0:T(8,128)} %get-tuple-element.54), channel_id=1, source_target_pairs={{4,8},{8,4},{12,16},{16,12},{20,24},{24,20},{5,9},{9,5},{13,17},{1... | collective-permute-start | bytes 245768 | tf_op jit(solution)/shard_map/ppermute | solution.py:40
  28.2 9.8 %all-to-all-start = ((f32[32,1,128]{2,1,0:T(1,128)}), f32[32,1,128]{2,1,0:T(1,128)S(1)}, u32[]{:S(2)}, u32[]{:S(2)}) async-start(f32[32,1,128]{2,1,0:T(1,128)} %bitcast.1), calls=%async_computation | async-start | bytes 32768 | tf_op jit(solution)/shard_map/all_to_all | solution.py:577
  39.3 6.4 %collective-permute-start.10 = (f32[4,8,8,128]{3,2,1,0:T(8,128)S(1)}, f32[4,8,8,128]{3,2,1,0:T(8,128)S(1)}, u32[]{:S(2)}, u32[]{:S(2)}) collective-permute-start(f32[4,8,8,128]{3,2,1,0:T(8,128)S(1)} %get-tuple-element.59), channel_id=1, source_target_pairs={{0,1},{1,0},{2,3},{3,2},{4,5},{5,4},{6,7},{7,6},{8,9},{9,8},{10,11... | collective-permute-start | bytes 393224 | tf_op jit(solution)/shard_map/ppermute | solution.py:40
  40.0 6.3 %collective-permute-start.11 = (f32[4,8,8,128]{3,2,1,0:T(8,128)S(1)}, f32[4,8,8,128]{3,2,1,0:T(8,128)S(1)}, u32[]{:S(2)}, u32[]{:S(2)}) collective-permute-start(f32[4,8,8,128]{3,2,1,0:T(8,128)S(1)} %get-tuple-element.60), channel_id=1, source_target_pairs={{1,2},{2,1},{5,6},{6,5},{9,10},{10,9},{13,14},{14,13},{17,18},{18,... | collective-permute-start | bytes 393224 | tf_op jit(solution)/shard_map/ppermute | solution.py:40
  42.2 4.3 %collective-permute-start.12 = (f32[4,4,16,128]{3,2,1,0:T(8,128)S(1)}, f32[4,4,16,128]{3,2,1,0:T(8,128)S(1)}, u32[]{:S(2)}, u32[]{:S(2)}) collective-permute-start(f32[4,4,16,128]{3,2,1,0:T(8,128)S(1)} %get-tuple-element.61), channel_id=1, source_target_pairs={{0,4},{4,0},{8,12},{12,8},{16,20},{20,16},{24,28},{28,24},{1,5},{5... | collective-permute-start | bytes 393224 | tf_op jit(solution)/shard_map/ppermute | solution.py:40
  43.4 7.4 %collective-permute-start.13 = (f32[4,4,16,128]{3,2,1,0:T(8,128)S(1)}, f32[4,4,16,128]{3,2,1,0:T(8,128)S(1)}, u32[]{:S(2)}, u32[]{:S(2)}) collective-permute-start(f32[4,4,16,128]{3,2,1,0:T(8,128)S(1)} %get-tuple-element.62), channel_id=1, source_target_pairs={{4,8},{8,4},{12,16},{16,12},{20,24},{24,20},{5,9},{9,5},{13,17},{1... | collective-permute-start | bytes 393224 | tf_op jit(solution)/shard_map/ppermute | solution.py:40
  51.1 8.2 %collective-permute-start.14 = (f32[64,128]{1,0:T(8,128)S(1)}, f32[64,128]{1,0:T(8,128)S(1)}, u32[]{:S(2)}, u32[]{:S(2)}) collective-permute-start(f32[64,128]{1,0:T(8,128)S(1)} %get-tuple-element.64), channel_id=1, source_target_pairs={{0,1},{1,0},{2,3},{3,2},{4,5},{5,4},{6,7},{7,6},{8,9},{9,8},{10,11... | collective-permute-start | bytes 98312 | tf_op jit(solution)/shard_map/ppermute | solution.py:40
  51.3 8.0 %collective-permute-start.15 = (f32[64,128]{1,0:T(8,128)S(1)}, f32[64,128]{1,0:T(8,128)S(1)}, u32[]{:S(2)}, u32[]{:S(2)}) collective-permute-start(f32[64,128]{1,0:T(8,128)S(1)} %get-tuple-element.65), channel_id=1, source_target_pairs={{1,2},{2,1},{5,6},{6,5},{9,10},{10,9},{13,14},{14,13},{17,18},{18,... | collective-permute-start | bytes 98312 | tf_op jit(solution)/shard_map/ppermute | solution.py:40
  55.4 4.0 %collective-permute-start.16 = (f32[64,128]{1,0:T(8,128)S(1)}, f32[64,128]{1,0:T(8,128)S(1)}, u32[]{:S(2)}, u32[]{:S(2)}) collective-permute-start(f32[64,128]{1,0:T(8,128)S(1)} %get-tuple-element.66), channel_id=1, source_target_pairs={{0,4},{4,0},{8,12},{12,8},{16,20},{20,16},{24,28},{28,24},{1,5},{5... | collective-permute-start | bytes 98312 | tf_op jit(solution)/shard_map/ppermute | solution.py:40
  55.4 5.6 %collective-permute-start.17 = (f32[64,128]{1,0:T(8,128)S(1)}, f32[64,128]{1,0:T(8,128)S(1)}, u32[]{:S(2)}, u32[]{:S(2)}) collective-permute-start(f32[64,128]{1,0:T(8,128)S(1)} %get-tuple-element.67), channel_id=1, source_target_pairs={{4,8},{8,4},{12,16},{16,12},{20,24},{24,20},{5,9},{9,5},{13,17},{1... | collective-permute-start | bytes 98312 | tf_op jit(solution)/shard_map/ppermute | solution.py:40
  61.3 7.5 %collective-permute-start.18 = (f32[4,8,8,128]{3,2,1,0:T(8,128)S(1)}, f32[4,8,8,128]{3,2,1,0:T(8,128)S(1)}, u32[]{:S(2)}, u32[]{:S(2)}) collective-permute-start(f32[4,8,8,128]{3,2,1,0:T(8,128)S(1)} %get-tuple-element.69), channel_id=1, source_target_pairs={{0,1},{1,0},{2,3},{3,2},{4,5},{5,4},{6,7},{7,6},{8,9},{9,8},{10,11... | collective-permute-start | bytes 393224 | tf_op jit(solution)/shard_map/ppermute | solution.py:40
  61.4 8.7 %collective-permute-start.19 = (f32[4,8,8,128]{3,2,1,0:T(8,128)S(1)}, f32[4,8,8,128]{3,2,1,0:T(8,128)S(1)}, u32[]{:S(2)}, u32[]{:S(2)}) collective-permute-start(f32[4,8,8,128]{3,2,1,0:T(8,128)S(1)} %get-tuple-element.70), channel_id=1, source_target_pairs={{1,2},{2,1},{5,6},{6,5},{9,10},{10,9},{13,14},{14,13},{17,18},{18,... | collective-permute-start | bytes 393224 | tf_op jit(solution)/shard_map/ppermute | solution.py:40
  64.5 5.6 %collective-permute-start.20 = (f32[4,4,16,128]{3,2,1,0:T(8,128)S(1)}, f32[4,4,16,128]{3,2,1,0:T(8,128)S(1)}, u32[]{:S(2)}, u32[]{:S(2)}) collective-permute-start(f32[4,4,16,128]{3,2,1,0:T(8,128)S(1)} %get-tuple-element.71), channel_id=1, source_target_pairs={{0,4},{4,0},{8,12},{12,8},{16,20},{20,16},{24,28},{28,24},{1,5},{5... | collective-permute-start | bytes 393224 | tf_op jit(solution)/shard_map/ppermute | solution.py:40
  64.5 7.3 %collective-permute-start.21 = (f32[4,4,16,128]{3,2,1,0:T(8,128)S(1)}, f32[4,4,16,128]{3,2,1,0:T(8,128)S(1)}, u32[]{:S(2)}, u32[]{:S(2)}) collective-permute-start(f32[4,4,16,128]{3,2,1,0:T(8,128)S(1)} %get-tuple-element.72), channel_id=1, source_target_pairs={{4,8},{8,4},{12,16},{16,12},{20,24},{24,20},{5,9},{9,5},{13,17},{1... | collective-permute-start | bytes 393224 | tf_op jit(solution)/shard_map/ppermute | solution.py:40
  68.4 8.2 %collective-permute-start.8 = (f32[8,16,128]{2,1,0:T(8,128)}, f32[8,16,128]{2,1,0:T(8,128)S(1)}, u32[]{:S(2)}, u32[]{:S(2)}) collective-permute-start(f32[8,16,128]{2,1,0:T(8,128)} %get-tuple-element.55), channel_id=1, source_target_pairs={{0,8},{8,0},{4,12},{12,4},{16,24},{24,16},{20,28},{28,20},{1,9},{9... | collective-permute-start | bytes 196616 | tf_op jit(solution)/shard_map/ppermute | solution.py:49
  68.8 18.0 %collective-permute-start.9 = (f32[8,16,128]{2,1,0:T(8,128)}, f32[8,16,128]{2,1,0:T(8,128)}, u32[]{:S(2)}, u32[]{:S(2)}) collective-permute-start(f32[8,16,128]{2,1,0:T(8,128)} %get-tuple-element.55), channel_id=1, source_target_pairs={{8,16},{16,8},{12,20},{20,12},{9,17},{17,9},{13,21},{21,13},{10,18... | collective-permute-start | bytes 196616 | tf_op jit(solution)/shard_map/ppermute | solution.py:49
  71.8 11.2 %copy-start.30 = (f32[4,9,9,256]{3,0,2,1:T(4,128)S(1)}, f32[4,9,9,256]{3,0,2,1:T(4,128)}, u32[]{:S(2)}) copy-start(f32[4,9,9,256]{3,0,2,1:T(4,128)} %param.15) | copy-start | bytes 995332
  73.5 19.5 %collective-permute-start.22 = (f32[64,128]{1,0:T(8,128)}, f32[64,128]{1,0:T(8,128)}, u32[]{:S(2)}, u32[]{:S(2)}) collective-permute-start(f32[64,128]{1,0:T(8,128)} %get-tuple-element.74), channel_id=1, source_target_pairs={{0,1},{1,0},{2,3},{3,2},{4,5},{5,4},{6,7},{7,6},{8,9},{9,8},{10,11... | collective-permute-start | bytes 98312 | tf_op jit(solution)/shard_map/ppermute | solution.py:40
  73.5 19.5 %collective-permute-start.23 = (f32[64,128]{1,0:T(8,128)}, f32[64,128]{1,0:T(8,128)}, u32[]{:S(2)}, u32[]{:S(2)}) collective-permute-start(f32[64,128]{1,0:T(8,128)} %get-tuple-element.75), channel_id=1, source_target_pairs={{1,2},{2,1},{5,6},{6,5},{9,10},{10,9},{13,14},{14,13},{17,18},{18,... | collective-permute-start | bytes 98312 | tf_op jit(solution)/shard_map/ppermute | solution.py:40
  76.5 16.5 %collective-permute-start.24 = (f32[64,128]{1,0:T(8,128)}, f32[64,128]{1,0:T(8,128)}, u32[]{:S(2)}, u32[]{:S(2)}) collective-permute-start(f32[64,128]{1,0:T(8,128)} %get-tuple-element.76), channel_id=1, source_target_pairs={{0,4},{4,0},{8,12},{12,8},{16,20},{20,16},{24,28},{28,24},{1,5},{5... | collective-permute-start | bytes 98312 | tf_op jit(solution)/shard_map/ppermute | solution.py:40
  77.2 15.8 %collective-permute-start.25 = (f32[64,128]{1,0:T(8,128)}, f32[64,128]{1,0:T(8,128)}, u32[]{:S(2)}, u32[]{:S(2)}) collective-permute-start(f32[64,128]{1,0:T(8,128)} %get-tuple-element.77), channel_id=1, source_target_pairs={{4,8},{8,4},{12,16},{16,12},{20,24},{24,20},{5,9},{9,5},{13,17},{1... | collective-permute-start | bytes 98312 | tf_op jit(solution)/shard_map/ppermute | solution.py:40
  (30 other events, 44.7 us)
where the time goes:
time: 96 us; the launch traced here: 95.1 us
  starting transfers between devices  51.5 us (54%)
  Pallas kernels  20.4 us (21%)
  waiting for transfers between devices  13.6 us (14%)
  local copies, waits for them, and re-layouts  8.31 us (9%)
  between operations  1.23 us (1%)
    ppermute x24, starting transfers between devices, swap(): return lax.ppermute(values, axis, pairs)  45.7 us
    pallas_call x13, Pallas kernels, call(): pl.pallas_call(kernel, out_shape=[jax.ShapeDtypeStruct(s, F32) for s in o...  20.4 us
    ppermute x24, waiting for transfers between devices, swap(): return lax.ppermute(values, axis, pairs)  8.52 us
    unnamed x76, local copies, waits for them, and re-layouts  8.31 us
    all_to_all x1, waiting for transfers between devices, shards(): lax.all_to_all(lists, ('gx', 'gz'), split_axis=0, concat_axis=0, tiled=True)  5.08 us
    all_to_all x1, starting transfers between devices, shards(): lax.all_to_all(lists, ('gx', 'gz'), split_axis=0, concat_axis=0, tiled=True)  4.2 us
  transfers between devices with their start and end apart: 27, of which 6 were waited for; matrix products, arithmetic and copies ran while one was open for 1% of the time, Pallas kernels for 16%

commit v1 on v0

v1 whole, which is shorter than its diff:
```python
import functools

import jax
import jax.numpy as jnp
from jax import lax
from jax.experimental import pallas as pl
from jax.experimental.pallas import tpu as pltpu
from jax.sharding import PartitionSpec as P

ORDERS = 4
RADIUS = 4
SUBSTEPS = 3
ZRIM = 8
LANES = 128
HEAD = 8
TIME_STEP = 0.5
STENCIL_WEIGHTS = (0.8, -0.2, 4.0 / 105.0, -1.0 / 280.0)
F32 = jnp.float32
BF16 = jnp.bfloat16


def call(kernel, name, outs, ins, scratch=(), flops=1_000_000, after=()):
    count, skip = len(ins), len(after)
    nbytes = 4 * sum(x.size for x in ins) + 4 * sum(functools.reduce(lambda m, n: m * n, s, 1) for s in outs)

    def body(*refs):
        kernel(*refs[:count], *refs[count + skip:])

    return pl.pallas_call(
        body,
        out_shape=[jax.ShapeDtypeStruct(s, F32) for s in outs],
        in_specs=[pl.BlockSpec(memory_space=pltpu.VMEM) for _ in ins]
        + [pl.BlockSpec(memory_space=pl.ANY) for _ in after],
        out_specs=[pl.BlockSpec(memory_space=pltpu.VMEM) for _ in outs],
        scratch_shapes=[pltpu.VMEM(s, F32) for s in scratch],
        compiler_params=pltpu.CompilerParams(vmem_limit_bytes=8 * 1024 * 1024),
        cost_estimate=pl.CostEstimate(flops=flops, bytes_accessed=nbytes, transcendentals=0),
        name=name,
    )(*ins, *after)


def swap(values, axis, odd, by=1):
    count = lax.axis_size(axis)
    pairs = []
    for i in range(count - by):
        if i // by % 2 == odd:
            pairs += [(i, i + by), (i + by, i)]
    return lax.ppermute(values, axis, pairs)


def exchange(xa, xb, za, zb):
    xb = swap(xb, "gx", 1)
    xa = swap(xa, "gx", 0)
    zb = swap(zb, "gz", 1)
    za = swap(za, "gz", 0)
    return za, zb, xa, xb


def sides(axis, by=1):
    parity = (lax.axis_index(axis) // by) & 1
    return 1 - parity, parity


def by_side(pair, axis, by=1):
    first = sides(axis, by)[0]
    return jnp.where(first == 0, pair[0], pair[1]), jnp.where(first == 1, pair[0], pair[1])


def halves(values):
    high = values.astype(BF16)
    return high, (values - high.astype(F32)).astype(BF16)


def dot3(left, right, dims=(((1,), (0,)), ((), ()))):
    lh, ll = halves(left)
    rh, rl = halves(right)
    mul = functools.partial(lax.dot_general, dimension_numbers=dims, preferred_element_type=F32)
    return mul(lh, rh) + (mul(lh, rl) + mul(ll, rh))


def dot_exact(left, right, dims=(((1,), (0,)), ((), ()))):
    return lax.dot_general(
        left, right, dims, precision=lax.Precision.HIGHEST, preferred_element_type=F32
    )


def flat_slots(table):
    rows, fields, slots = table.shape
    lane = lax.broadcasted_iota(jnp.int32, (slots, LANES), 1)
    place = lax.broadcasted_iota(jnp.int32, (slots, LANES), 0)
    spread = jnp.where(lane % slots == place, 1.0, 0.0).astype(F32)
    lane = lax.broadcasted_iota(jnp.int32, (fields, LANES), 1)
    flat = jnp.zeros((fields, LANES), F32)
    for r in range(rows):
        flat = jnp.where(lane // slots == r, dot_exact(table[r].astype(F32), spread), flat)
    return flat


def pack_x(out, at, source, side):
    start = side * (source.shape[1] - RADIUS)
    out[pl.ds(at, source.shape[0])] = source[:, pl.ds(start, RADIUS)]


def pack_z(out, at, source, side):
    start = pl.multiple_of(side * (source.shape[2] - ZRIM), ZRIM)
    out[pl.ds(at, source.shape[0])] = source[:, :, pl.ds(start, ZRIM), :]


def widen(ext, center, za, zb, xa, xb, first=0, block=0):
    fields, nx, nz = center.shape[0], center.shape[1], center.shape[2]
    ext[:, RADIUS:RADIUS + nx, ZRIM:ZRIM + nz] = center[...]
    for got, side in zip((xa, xb), sides("gx")):
        place = pl.ds(side * (nx + RADIUS), RADIUS)
        if block:
            ext[0, place, ZRIM:ZRIM + nz] = got[(block - 1) * (1 - side)]
            ext[1:, place, ZRIM:ZRIM + nz] = got[block:block + fields - 1]
        else:
            skip = xa.shape[0] - za.shape[0] if first else 0
            ext[:, place, ZRIM:ZRIM + nz] = got[first + skip:first + skip + fields]
    for got, side in zip((za, zb), sides("gz")):
        start = pl.multiple_of(side * (nz + ZRIM), ZRIM)
        ext[:, RADIUS:RADIUS + nx, pl.ds(start, ZRIM)] = got[first:first + fields]


def d1(load, x, lo, hi):
    total = None
    for m, w in enumerate(STENCIL_WEIGHTS, 1):
        term = w * (load(x + m, lo, hi) - load(x - m, lo, hi))
        total = term if total is None else total + term
    return total


def d2(load, x, lo, hi):
    total = None
    for m, w in enumerate(STENCIL_WEIGHTS, 1):
        term = w * (load(x, lo + m, hi + m) - load(x, lo - m, hi - m))
        total = term if total is None else total + term
    return total


def d3(values):
    width = values.shape[1]
    lane = lax.broadcasted_iota(jnp.int32, (1, width), 1)
    total = None
    for m, w in enumerate(STENCIL_WEIGHTS, 1):
        ahead = jnp.where(lane < width - m, w, 0.0) * pltpu.roll(values, width - m, 1)
        behind = jnp.where(lane >= m, w, 0.0) * pltpu.roll(values, m, 1)
        term = ahead - behind
        total = term if total is None else total + term
    return total


def field(ref, c):
    return lambda x, lo, hi: ref[c, x, lo:hi, :]


def plane(ref):
    return lambda x, lo, hi: ref[x, lo:hi, :]


def arrived(lists, da, band, reach, slots):
    lane = lax.broadcasted_iota(jnp.int32, (1, LANES), 1)
    got = jnp.zeros((1, LANES), F32)
    for r in range(reach):
        row = lists[da - (r - reach // 2) + 3][band:band + 1]
        got = jnp.where((lane & (LANES // 2 - 1)) // slots == r, row, got)
    return got, pltpu.roll(got, LANES // 2, 1)


def cell_masks(cells, rows):
    cells = cells.astype(jnp.int32)
    place = lax.broadcasted_iota(jnp.int32, (rows, LANES), 0)
    third = lax.broadcasted_iota(jnp.int32, (LANES, LANES), 0)
    return cells // LANES == place, cells % LANES == third


def raw_rims_kernel(air, wind, xa, xb, za, zb):
    fields, nx = air.shape[:2]
    parts = nx // RADIUS
    for out, side in zip((xa, xb), sides("gx")):
        start = side * (nx - RADIUS)
        for part in range(parts):
            out[part] = air[0, part * RADIUS:(part + 1) * RADIUS]
        out[parts:parts + fields - 1] = air[1:, pl.ds(start, RADIUS)]
        pack_x(out, parts + fields - 1, wind, side)
    for out, side in zip((za, zb), sides("gz")):
        pack_z(out, 0, air, side)
        pack_z(out, fields, wind, side)


def lanes(at):
    return pl.ds(at if isinstance(at, int) else pl.multiple_of(at, LANES), LANES)


def jacobian_step(jac, rot, emit):
    quants, dims, width = jac.shape[1:]
    rows = rot.shape[0] // dims

    def half(h, carry):
        at = h * LANES
        acc = [None] * quants
        for d in range(dims):
            for q in range(quants):
                turned = rot[d * rows:(d + 1) * rows, lanes(q * width + at)]
                for p in range(quants):
                    term = jac[p, q, d:d + 1, lanes(at)] * turned
                    acc[p] = term if acc[p] is None else acc[p] + term
        for p in range(quants):
            emit(p, at, acc[p])
        return carry

    lax.fori_loop(0, width // LANES, half, 0)


def rotate(rot, matrix, source, quants, width):
    for q in range(quants):
        cut = slice(q * width, (q + 1) * width)
        rot[:, cut] = dot3(matrix[...], source[:, cut])


def take_slots(tiles, index):
    low = index % LANES
    high = index // LANES
    got = None
    for s, tile in enumerate(tiles):
        picked = jnp.take_along_axis(tile, low, axis=1, mode="promise_in_bounds")
        got = picked if got is None else jnp.where(high == s, picked, got)
    return got


def predict_kernel(
    state, jac, stiff, trace, sends, smap, normals,
    integral, traces, own, xa, xb, za, zb, row,
    cur, rot, sp, tp, picked,
):
    quants, basis, width = state.shape
    pad = integral.shape[0]
    face_basis, faces = trace.shape[:2]
    dims = stiff.shape[0]
    sp[...] = jnp.zeros_like(sp)
    tp[...] = jnp.zeros_like(tp)
    cur[...] = jnp.zeros_like(cur)
    for d in range(dims):
        sp[d * pad:d * pad + basis, 0:basis] = stiff[d]
    for f in range(faces):
        for j in range(face_basis):
            tp[f * 16 + j:f * 16 + j + 1, 0:basis] = trace[j, f:f + 1, :]
    for q in range(quants):
        cur[0:basis, q * width:(q + 1) * width] = state[q]
    integral[...] = TIME_STEP * cur[0:pad, :]

    def degree(k, weight):
        weight = jnp.where(k == 1, TIME_STEP**2 / 2, jnp.where(k == 2, TIME_STEP**3 / 6, TIME_STEP**4 / 24))
        rotate(rot, sp, cur, quants, width)

        def emit(p, at, value):
            cut = lanes(p * width + at)
            cur[0:pad, cut] = -value
            integral[:, cut] = integral[:, cut] - weight * value

        jacobian_step(jac, rot, emit)
        return weight

    lax.fori_loop(1, ORDERS, degree, F32(0))
    for q in range(quants):
        cut = slice(q * width, (q + 1) * width)
        done = dot3(tp[:, 0:pad], integral[:, cut])
        for f in range(faces):
            traces[q, :, f * width:(f + 1) * width] = done[f * 16:(f + 1) * 16]
    slots = flat_slots(smap)
    wanted = [jnp.broadcast_to(sends[d:d + 1, :], (16, LANES)) for d in range(4)]
    wanted.append(jnp.broadcast_to(slots[0:1].astype(jnp.int32), (16, LANES)))
    tiles_in = faces * width // LANES

    def gather(q, carry):
        tiles = [traces[q, :, s * LANES:(s + 1) * LANES] for s in range(tiles_in)]
        for d in range(4):
            picked[d, q] = take_slots(tiles, wanted[d])
        own[q] = take_slots(tiles, wanted[4])
        return carry

    lax.fori_loop(0, quants, gather, 0)
    for axis, base, outs in (("gx", 0, (xa, xb)), ("gz", 2, (za, zb))):
        for out, side in zip(outs, sides(axis)):
            for q in range(quants):
                out[q * 8:q * 8 + 8, :] = picked[base + side, q, 0:8, :]
                out[quants * 8 + q * 2:quants * 8 + q * 2 + 2, :] = picked[base + side, q, 8:face_basis, :]
            out[quants * face_basis:, :] = jnp.zeros((out.shape[0] - quants * face_basis, LANES), F32)
    normal = flat_slots(normals)
    speed = jnp.zeros((1, LANES), F32)
    for c in range(3):
        mean = jnp.sum(own[6 + c, 0:face_basis, :], axis=0, keepdims=True) * (1.0 / face_basis)
        speed = speed + normal[c:c + 1] * mean
    lane = lax.broadcasted_iota(jnp.int32, (1, LANES), 1)
    cells = pltpu.roll(slots[1:2], LANES // 2, 1)
    row[...] = jnp.where(lane < LANES // 2, slots[2:3] * speed, cells)


def pressure_rows(ext, wind, medium, x, nz):
    lo, hi = ZRIM, ZRIM + nz
    xe = x + RADIUS
    pressure = field(ext, 0)
    here = pressure(xe, lo, hi)
    divergence = d1(field(ext, 1), xe, lo, hi) + d2(field(ext, 2), xe, lo, hi) + d3(ext[3, xe, lo:hi, :])
    moved = (
        wind[0, x] * d1(pressure, xe, lo, hi)
        + wind[1, x] * d2(pressure, xe, lo, hi)
        + wind[2, x] * d3(here)
    )
    return here - medium[0, x] * divergence - moved


def pack_pressure(center, xs, zs, at=0):
    nx, nz, ny = center.shape[1:]
    for out, side in zip(xs, sides("gx")):
        start = side * (nx - RADIUS)
        out[at:at + RADIUS * nz, :] = center[0, pl.ds(start, RADIUS)].reshape(RADIUS * nz, ny)
    for out, side in zip(zs, sides("gz")):
        start = pl.multiple_of(side * (nz - ZRIM), ZRIM)
        out[at:at + nx * ZRIM, :] = center[0, :, pl.ds(start, ZRIM), :].reshape(nx * ZRIM, ny)


def widen_pressure(ext, center, za, zb, xa, xb, at=0):
    nx, nz, ny = center.shape
    ext[RADIUS:RADIUS + nx, ZRIM:ZRIM + nz] = center[...]
    for got, side in zip((xa, xb), sides("gx")):
        ext[pl.ds(side * (nx + RADIUS), RADIUS), ZRIM:ZRIM + nz] = got[at:at + RADIUS * nz, :].reshape(RADIUS, nz, ny)
    for got, side in zip((za, zb), sides("gz")):
        start = pl.multiple_of(side * (nz + ZRIM), ZRIM)
        ext[RADIUS:RADIUS + nx, pl.ds(start, ZRIM)] = got[at:at + nx * ZRIM, :].reshape(nx, ZRIM, ny)


def raw_pressure_kernel(air, wind, medium, za, zb, xa, xb, tza, tzb, row, pressure, oza, ozb, ext):
    nx, nz, ny = air.shape[1:]
    widen(ext, air, za, zb, xa, xb, block=nx // RADIUS)
    for x in range(nx):
        pressure[0, x] = pressure_rows(ext, wind, medium, x, nz)
    pack_pressure(pressure, (), (oza, ozb), HEAD)
    for out, sent in zip((oza, ozb), (tza, tzb)):
        out[0:HEAD, :] = jnp.broadcast_to(row[...], (HEAD, LANES))
        out[out.shape[0] - sent.shape[0]:, :] = sent[...]


def merge_kernel(air, raw, txa, txb, za, zb, row, oxa, oxb, far, farther):
    nx, nz, ny = air.shape[1:]
    low, high = by_side((za[0:1, :], zb[0:1, :]), "gz")
    place = lax.broadcasted_iota(jnp.int32, (HEAD, LANES), 0)
    lists = jnp.where(place == 0, row[...], jnp.where(place == 1, low, jnp.where(place == 2, high, 0.0)))
    pack_pressure(raw, (oxa, oxb), (), HEAD)
    for out, sent in zip((oxa, oxb), (txa, txb)):
        out[0:HEAD, :] = lists
        out[out.shape[0] - sent.shape[0]:, :] = sent[...]
    far[0:HEAD, :] = lists
    far[HEAD:, :] = air[0].reshape(nx * nz, ny)
    farther[...] = lists


def advection_kernel(block, air, wind, za, zb, xa, xb, moved, ext):
    nx, nz, ny = air.shape[1:]
    widen(ext, air, za, zb, xa, xb, block=block)
    lo, hi = ZRIM, ZRIM + nz
    for x in range(nx):
        xe = x + RADIUS
        for c in range(3):
            load = field(ext, 1 + c)
            moved[c, x] = (
                wind[0, x] * d1(load, xe, lo, hi)
                + wind[1, x] * d2(load, xe, lo, hi)
                + wind[2, x] * d3(load(xe, lo, hi))
            )


def velocities(out, center, moved, medium, wide, nx, nz):
    lo, hi = ZRIM, ZRIM + nz
    load = plane(wide)
    for x in range(nx):
        xe = x + RADIUS
        slopes = (d1(load, xe, lo, hi), d2(load, xe, lo, hi), d3(load(xe, lo, hi)))
        out[0, x] = load(xe, lo, hi)
        for c in range(3):
            out[1 + c, x] = center[1 + c, x] - medium[1, x] * slopes[c] - moved[c, x]


def pack_air(out, xa, xb, za, zb):
    for rim, side in zip((xa, xb), sides("gx")):
        pack_x(rim, 0, out, side)
    for rim, side in zip((za, zb), sides("gz")):
        pack_z(rim, 0, out, side)


def injected_kernel(
    air, wind, medium, raw, moved, wza, wzb, wxa, wxb, pza, pzb, pxa, pxb, farther, f2a, f2b, f3a, f3b, smap,
    out, oxa, oxb, oza, ozb, spread, wide, wide_wind,
):
    nx, nz, ny = air.shape[1:]
    reach, _, slots = smap.shape
    used = lax.broadcasted_iota(jnp.int32, (nx * nz, LANES), 1) < reach * slots
    lists = [None, None, None, farther[...], None, None, None]
    for by, pair in ((1, (pxa, pxb)), (2, (f2a, f2b)), (3, (f3a, f3b))):
        lists[3 - by], lists[3 + by] = by_side([got[0:HEAD, :] for got in pair], "gx", by)
    for da in range(3):
        for db in range(3):
            speed, cells = arrived(lists, da - 1, (1, 0, 2)[db], reach, slots)
            row_mask, third_mask = cell_masks(cells, nx * nz)
            high, low = halves(jnp.where(row_mask & used, speed, 0.0))
            columns = jnp.where(third_mask, 1.0, 0.0).astype(BF16)
            mul = functools.partial(
                lax.dot_general, dimension_numbers=(((1,), (1,)), ((), ())), preferred_element_type=F32
            )
            block = mul(high, columns) + mul(low, columns)
            spread[da * nx:(da + 1) * nx, db * nz:(db + 1) * nz] = block.reshape(nx, nz, ny)
    widen(wide_wind, wind, wza, wzb, wxa, wxb, first=air.shape[0])
    widen_pressure(wide, raw.at[0], pza, pzb, pxa, pxb, HEAD)
    load = plane(spread)
    for x in range(nx + 2 * RADIUS):
        xs = x + nx - RADIUS
        if RADIUS <= x < RADIUS + nx:
            lo, hi = 0, nz + 2 * ZRIM
        else:
            lo, hi = ZRIM, ZRIM + nz
        slo, shi = lo + nz - ZRIM, hi + nz - ZRIM
        here = load(xs, slo, shi)
        turned = (
            wide_wind[0, x, lo:hi, :] * d1(load, xs, slo, shi)
            + wide_wind[1, x, lo:hi, :] * d2(load, xs, slo, shi)
            + wide_wind[2, x, lo:hi, :] * d3(here)
        )
        wide[x, lo:hi, :] = wide[x, lo:hi, :] + (here - turned)
    velocities(out, air, moved, medium, wide, nx, nz)
    pack_air(out, oxa, oxb, oza, ozb)


def pressure_kernel(air, wind, medium, za, zb, xa, xb, pressure, oxa, oxb, oza, ozb, ext):
    nx, nz, ny = air.shape[1:]
    widen(ext, air, za, zb, xa, xb)
    for x in range(nx):
        pressure[0, x] = pressure_rows(ext, wind, medium, x, nz)
    pack_pressure(pressure, (oxa, oxb), (oza, ozb))


def velocity_kernel(air, pressure, medium, moved, za, zb, xa, xb, out, *rest):
    nx, nz, ny = air.shape[1:]
    wide = rest[-1]
    widen_pressure(wide, pressure.at[0], za, zb, xa, xb)
    velocities(out, air, moved, medium, wide, nx, nz)
    if len(rest) > 1:
        pack_air(out, *rest[:-1])


def volume_kernel(state, integral, jac, stiff, out, rot, sp):
    quants, basis, width = state.shape
    pad = integral.shape[0]
    dims = stiff.shape[0]
    sp[...] = jnp.zeros_like(sp)
    place = lax.broadcasted_iota(jnp.int32, (basis, basis), 0)
    other = lax.broadcasted_iota(jnp.int32, (basis, basis), 1)
    unit = jnp.where(place == other, 1.0, 0.0).astype(F32)
    for d in range(dims):
        sp[d * pad:d * pad + basis, 0:basis] = dot_exact(unit, stiff[d], (((1,), (1,)), ((), ())))
    for q in range(quants):
        cut = slice(q * width, (q + 1) * width)
        rot[:, cut] = dot3(sp[:, 0:pad], integral[:, cut])

    def emit(p, at, value):
        out[p, :, lanes(at)] = state[p, :, lanes(at)] + value[0:basis]

    jacobian_step(jac, rot, emit)


def flux_kernel(
    first, faces, base, traces, own, solvers, lift, neighbours, smap, za, zb, xa, xb, air, nxa, nxb, fxa, fxb,
    out, tiles, flux, lp,
):
    quants, basis, width = base.shape
    face_basis = lift.shape[0]
    reach, _, slots = smap.shape
    nx, nz, ny = air.shape[1:]
    rows = nx * nz
    lane = lax.broadcasted_iota(jnp.int32, (1, LANES), 1)
    flat = flat_slots(smap)
    row_mask, third_mask = cell_masks(flat[1:2], rows)
    columns = jnp.where(third_mask, 1.0, 0.0).astype(BF16)
    near = by_side([got[0:nx // RADIUS].reshape(rows, ny) for got in (nxa, nxb)], "gx")
    far = by_side([got[HEAD:, :] for got in (fxa, fxb)], "gx", 2)
    blocks = [far[0], near[0], air[0].reshape(rows, ny), near[1], far[1]]
    replies = jnp.zeros((1, LANES), F32)
    for r in range(reach):
        high, low = halves(blocks[r])
        looked = jnp.dot(high, columns, preferred_element_type=F32)
        looked = looked + jnp.dot(low, columns, preferred_element_type=F32)
        found = jnp.sum(jnp.where(row_mask, looked, 0.0), axis=0, keepdims=True)
        replies = jnp.where(lane // slots == r, found, replies)
    replies = replies * flat[2:3]
    skip = xa.shape[0] - sent_rows(quants, face_basis)
    for axis, base_tile, gots in (("gx", 0, (xa, xb)), ("gz", 2, (za, zb))):
        for got, side in zip(gots, sides(axis)):
            for q in range(quants):
                tiles[q, base_tile + side, 0:8, :] = got[skip + q * 8:skip + q * 8 + 8, :]
                at = skip + quants * 8 + q * 2
                tiles[q, base_tile + side, 8:face_basis, :] = got[at:at + 2, :]
                tiles[q, base_tile + side, face_basis:, :] = jnp.zeros((16 - face_basis, LANES), F32)
    for q in range(quants):
        tiles[q, 4] = -2.0 * replies - own[q] if q < 3 else own[q]
    lp[...] = jnp.zeros_like(lp)
    for f in range(faces):
        for j in range(face_basis):
            lp[f * 16 + j:f * 16 + j + 1, 0:basis] = lift[j, first + f:first + f + 1, :]
    unit = lax.broadcasted_iota(jnp.int32, (lp.shape[1], lp.shape[1]), 0) == lax.broadcasted_iota(
        jnp.int32, (lp.shape[1], lp.shape[1]), 1
    )
    lifted = dot_exact(jnp.where(unit, 1.0, 0.0).astype(F32), lp[...], (((1,), (1,)), ((), ())))
    local = traces.shape[2] // LANES
    halves_in = width // LANES

    def one(h, carry):
        at = h * LANES
        for f in range(faces):
            index = jnp.broadcast_to(neighbours[first + f:first + f + 1, lanes(at)], (16, LANES))
            acc = [None] * quants
            for q in range(quants):
                pool = [traces[q, :, s * LANES:(s + 1) * LANES] for s in range(local)]
                pool += [tiles[q, s] for s in range(5)]
                mine = traces[q, :, lanes((first + f) * width + at)]
                jump = take_slots(pool, index) - mine
                for p in range(quants):
                    term = solvers[p, q, first + f:first + f + 1, lanes(at)] * jump
                    acc[p] = term if acc[p] is None else acc[p] + term
            for p in range(quants):
                flux[f * 16:(f + 1) * 16, lanes(p * width + at)] = acc[p]
        return carry

    lax.fori_loop(0, halves_in, one, 0)
    for p in range(quants):
        cut = slice(p * width, (p + 1) * width)
        out[p] = base[p] + dot3(lifted, flux[:, cut])[0:basis]


def sent_rows(quants, face_basis):
    return -(-quants * face_basis // 8) * 8


def shards(
    solid_state, jacobians, flux_solvers, stiffness, trace_matrix, lift_matrix,
    neighbours, send_faces, surface_map, surface_normals, air_state, wind_field, air_medium,
):
    quants, basis, width = solid_state.shape
    faces, face_basis = trace_matrix.shape[0], trace_matrix.shape[1]
    dims = stiffness.shape[0]
    nx, nz, ny = air_state.shape[1:]
    jacobians = jnp.transpose(jacobians, (1, 2, 0, 3))
    flux_solvers = jnp.transpose(flux_solvers, (1, 2, 0, 3))
    trace_matrix = jnp.transpose(trace_matrix, (1, 0, 2))
    lift_matrix = jnp.transpose(lift_matrix, (2, 0, 1))
    surface_map = jnp.transpose(surface_map, (1, 0, 2))
    surface_normals = jnp.transpose(surface_normals, (1, 0, 2))
    pad = -(-basis // 8) * 8
    pad_k = -(-basis // 16) * 16
    parts = nx // RADIUS
    rim_x = (parts + 6, RADIUS, nz, ny)
    rim_z = (7, nx, ZRIM, ny)
    ext = (4, nx + 2 * RADIUS, nz + 2 * ZRIM, ny)
    wide = ext[1:]
    block = (1, nx, nz, ny)

    xa, xb, za, zb = call(raw_rims_kernel, "raw_rims", [rim_x, rim_x, rim_z, rim_z], [air_state, wind_field])
    rims = exchange(xa, xb, za, zb)

    sent = (sent_rows(quants, face_basis), LANES)
    integral, traces, own, txa, txb, tza, tzb, row = call(
        predict_kernel, "predict",
        [(pad, quants * width), (quants, 16, faces * width), (quants, 16, LANES), sent, sent, sent, sent,
         (1, LANES)],
        [solid_state, jacobians, stiffness, trace_matrix, send_faces, surface_map, surface_normals],
        [(pad_k, quants * width), (dims * pad, quants * width), (dims * pad, pad_k), (faces * 16, pad_k),
         (4, quants, 16, LANES)],
        flops=40_000_000,
    )
    both_x = (HEAD + RADIUS * nz + sent[0], LANES)
    both_z = (HEAD + nx * ZRIM + sent[0], LANES)
    raw, za, zb = call(
        raw_pressure_kernel, "raw_pressure", [block, both_z, both_z],
        [air_state, wind_field, air_medium, *rims, tza, tzb, row], [ext],
    )
    both_za, both_zb = swap(za, "gz", 0), swap(zb, "gz", 1)
    (moved,) = call(
        functools.partial(advection_kernel, parts), "advection", [(3, nx, nz, ny)],
        [air_state, wind_field, *rims], [ext], flops=10_000_000, after=[za],
    )
    (volume,) = call(
        volume_kernel, "volume", [solid_state.shape], [solid_state, integral, jacobians, stiffness],
        [(dims * pad, quants * width), (dims * pad, pad_k)], flops=10_000_000, after=[za],
    )
    xa, xb, far, farther = call(
        merge_kernel, "merge", [both_x, both_x, (HEAD + nx * nz, LANES), (HEAD, LANES)],
        [air_state, raw, txa, txb, both_za, both_zb, row],
    )
    both = (both_za, both_zb, swap(xa, "gx", 0), swap(xb, "gx", 1))
    far2 = swap(far, "gx", 0, 2), swap(far, "gx", 1, 2)
    far3 = swap(farther, "gx", 0, 3), swap(farther, "gx", 1, 3)

    raw_xa, raw_xb = rims[2:]
    rim_x = (4, RADIUS, nz, ny)
    rim_z = (4, nx, ZRIM, ny)
    air, xa, xb, za, zb = call(
        injected_kernel, "injected",
        [air_state.shape, rim_x, rim_x, rim_z, rim_z],
        [air_state, wind_field, air_medium, raw, moved, *rims, *both, farther, *far2, *far3, surface_map],
        [(3 * nx, 3 * nz, ny), wide, (3,) + wide], after=[volume],
    )
    half = faces // 2
    solid = volume
    for substep in range(1, SUBSTEPS):
        rims = exchange(xa, xb, za, zb)
        (solid,) = call(
            functools.partial(flux_kernel, (substep - 1) * half, half), "flux", [solid_state.shape],
            [solid, traces, own, flux_solvers, lift_matrix, neighbours, surface_map, *both,
             air_state, raw_xa, raw_xb, *far2],
            [(quants, 5, 16, LANES), (half * 16, quants * width), (half * 16, pad)], flops=20_000_000,
            after=[xa],
        )
        pressure, xa, xb, za, zb = call(
            pressure_kernel, "pressure",
            [block, (RADIUS * nz, ny), (RADIUS * nz, ny), (nx * ZRIM, ny), (nx * ZRIM, ny)],
            [air, wind_field, air_medium, *rims], [ext], after=[solid],
        )
        rises = exchange(xa, xb, za, zb)
        (moved,) = call(
            functools.partial(advection_kernel, 0), "advection", [(3, nx, nz, ny)],
            [air, wind_field, *rims], [ext], flops=10_000_000, after=[xa],
        )
        last = substep == SUBSTEPS - 1
        outs = [air_state.shape] + ([] if last else [rim_x, rim_x, rim_z, rim_z])
        done = call(
            velocity_kernel, "velocity", outs, [air, pressure, air_medium, moved, *rises], [wide]
        )
        air = done[0]
        if not last:
            xa, xb, za, zb = done[1:]
    return (solid, air)


def solution(mesh):
    in_specs = (
        P(None, None, ("gx", "gz")),
        P(None, None, None, ("gx", "gz")),
        P(None, None, None, ("gx", "gz")),
        P(),
        P(),
        P(),
        P(None, ("gx", "gz")),
        P(None, ("gx", "gz")),
        P(None, None, ("gx", "gz")),
        P(None, None, ("gx", "gz")),
        P(None, "gx", "gz", None),
        P(None, "gx", "gz", None),
        P(None, "gx", "gz", None),
    )
    out_specs = (P(None, None, ("gx", "gz")), P(None, "gx", "gz", None))
    return jax.shard_map(shards, mesh=mesh, in_specs=in_specs, out_specs=out_specs, check_vma=False)
```

time: 96 us -> 93.4 us (0.973)
  the two profiles are of different devices: /device:TPU:5 before, /device:TPU:0 now
where the time goes in v1:
time: 93.4 us; the launch traced here: 91.8 us
  starting transfers between devices  59 us (63%)
  Pallas kernels  16.1 us (17%)
  waiting for transfers between devices  11.3 us (12%)
  local copies, waits for them, and re-layouts  4.42 us (5%)
  between operations  1.04 us (1%)
    ppermute x28, starting transfers between devices, swap(): return lax.ppermute(values, axis, pairs)  59 us
    pallas_call x15, Pallas kernels, call(): pl.pallas_call(body, out_shape=[jax.ShapeDtypeStruct(s, F32) for s in out...  16.1 us
    ppermute x28, waiting for transfers between devices, swap(): return lax.ppermute(values, axis, pairs)  11.3 us
    unnamed x32, local copies, waits for them, and re-layouts  4.42 us
  transfers between devices with their start and end apart: 28, of which 6 were waited for; matrix products, arithmetic and copies ran while one was open for 0% of the time, Pallas kernels for 13%

profile of v1, /device:TPU:0, one launch (start us, length us, event | category | flops | bytes accessed | tf_op | source)
XLA Modules:
  0.0 91.8 jit_solution(2532272192041871375)
XLA Ops:
  0.6 0.9 %copy-done = f32[4,8,16,128]{3,2,1,0:T(8,128)S(1)} copy-done((f32[4,8,16,128]{3,2,1,0:T(8,128)S(1)}, f32[4,8,16,128]{3,2,1,0:T(8,128)}, u32[]{:S(2)}) %copy-start) | copy-done | bytes 262168
  1.6 0.9 %copy-done.2 = f32[3,8,16,128]{3,2,1,0:T(8,128)S(1)} copy-done((f32[3,8,16,128]{3,2,1,0:T(8,128)S(1)}, f32[3,8,16,128]{3,2,1,0:T(8,128)}, u32[]{:S(2)}) %copy-start.2) | copy-done | bytes 196632
  2.6 3.0 %collective-permute-start.2 = (f32[8,4,16,128]{3,2,1,0:T(8,128)S(1)}, f32[8,4,16,128]{3,2,1,0:T(8,128)S(1)}, u32[]{:S(2)}, u32[]{:S(2)}) collective-permute-start(f32[8,4,16,128]{3,2,1,0:T(8,128)S(1)} %get-tuple-element.44), channel_id=1, source_target_pairs={{0,4},{4,0},{8,12},{12,8},{16,20},{20,16},{24,28},{28,24},{1,5},{5... | collective-permute-start | bytes 786440 | tf_op jit(solution)/shard_map/ppermute | solution.py:48
  5.6 0.7 collective-permute-start.3
  6.4 0.7 collective-permute-start.1
  7.8 0.9 %copy-done.8 = f32[9,20,256]{2,1,0:T(8,128)S(1)} copy-done((f32[9,20,256]{2,1,0:T(8,128)S(1)}, f32[9,20,256]{2,1,0:T(8,128)}, u32[]{:S(2)}) %copy-start.8) | copy-done | bytes 184344
  8.7 5.0 %predict.1 = (f32[24,2304]{1,0:T(8,128)S(1)}, f32[9,16,1024]{2,1,0:T(8,128)S(1)}, f32[9,16,128]{2,1,0:T(8,128)S(1)}, f32[96,128]{1,0:T(8,128)S(1)}, f32[96,128]{...) custom-call(f32[9,20,256]{2,1,0:T(8,128)S(1)} %copy-done.8, ...), custom_call_target="tpu_custom_call" | custom-call | flops 40000000 | bytes 1526016 | tf_op jit(solution)/shard_map/predict/pallas_call | solution.py:29
  13.7 3.1 %collective-permute-done.2.refs_5_.refs_4_.refs_7_.refs_12_ = f32[8,4,16,128]{3,2,1,0:T(8,128)S(1)} collective-permute-done((f32[8,4,16,128]{3,2,1,0:T(8,128)S(1)}, f32[8,4,16,128]{3,2,1,0:T(8,128)S(1)}, u32[]{:S(2)}, u32[]{:S(2)}) %collective-permute-start.2) | collective-permute-done | bytes 262176 | tf_op jit(solution)/shard_map/ppermute | solution.py:48
  17.2 0.7 collective-permute-start.5
  17.9 2.9 %collective-permute-start.4 = (f32[168,128]{1,0:T(8,128)S(1)}, f32[168,128]{1,0:T(8,128)S(1)}, u32[]{:S(2)}, u32[]{:S(2)}) collective-permute-start(f32[168,128]{1,0:T(8,128)S(1)} %get-tuple-element.49.refs_4_.refs_6_), channel_id=1, source_target_pairs={{0,1},{1,0},{2,3},{3,2},{4,5},{5,4},{6,7},{7,6},{8,9},{9,8},{10,11... | collective-permute-start | bytes 258056 | tf_op jit(solution)/shard_map/ppermute | solution.py:48
  20.8 0.9 %collective-permute-done.4.refs_4_.refs_9_.refs_7_ = f32[168,128]{1,0:T(8,128)S(1)} collective-permute-done((f32[168,128]{1,0:T(8,128)S(1)}, f32[168,128]{1,0:T(8,128)S(1)}, u32[]{:S(2)}, u32[]{:S(2)}) %collective-permute-start.4) | collective-permute-done | bytes 86048 | tf_op jit(solution)/shard_map/ppermute | solution.py:48
  21.8 3.1 %collective-permute-start.6 = (f32[168,128]{1,0:T(8,128)S(1)}, f32[168,128]{1,0:T(8,128)S(1)}, u32[]{:S(2)}, u32[]{:S(2)}) collective-permute-start(f32[168,128]{1,0:T(8,128)S(1)} %get-tuple-element.56), channel_id=1, source_target_pairs={{0,4},{4,0},{8,12},{12,8},{16,20},{20,16},{24,28},{28,24},{1,5},{5... | collective-permute-start | bytes 258056 | tf_op jit(solution)/shard_map/ppermute | solution.py:48
  26.2 5.7 %collective-permute-start.8 = (f32[136,128]{1,0:T(8,128)S(1)}, f32[136,128]{1,0:T(8,128)S(1)}, u32[]{:S(2)}, u32[]{:S(2)}) collective-permute-start(f32[136,128]{1,0:T(8,128)S(1)} %get-tuple-element.58), channel_id=1, source_target_pairs={{0,8},{8,0},{4,12},{12,4},{16,24},{24,16},{20,28},{28,20},{1,9},{9... | collective-permute-start | bytes 208904 | tf_op jit(solution)/shard_map/ppermute | solution.py:48
  32.6 9.4 %collective-permute-start.10 = (f32[8,128]{1,0:T(8,128)S(1)}, f32[8,128]{1,0:T(8,128)S(1)}, u32[]{:S(2)}, u32[]{:S(2)}) collective-permute-start(f32[8,128]{1,0:T(8,128)S(1)} %get-tuple-element.59.refs_13_), channel_id=1, source_target_pairs={{0,12},{12,0},{4,16},{16,4},{8,20},{20,8},{1,13},{13,1},{5,17},{17... | collective-permute-start | bytes 12296 | tf_op jit(solution)/shard_map/ppermute | solution.py:48
  42.0 1.3 %volume.1.refs_19_.refs_0_ = f32[9,20,256]{2,1,0:T(8,128)S(1)} custom-call(f32[9,20,256]{2,1,0:T(8,128)S(1)} %copy-done.8, f32[24,2304]{1,0:T(8,128)S(1)} %get-tuple-element.41.refs_1_, f32[9,9,3,256]{3,2,1,0:T(4,128)S(1)} %bitcast.9, f32[3,20,20]{2,1,0:T(8,128)S(1)} %copy-done.10, f32[168,128]{1,0:T(8,128)S(1)} %get-tuple-element.49.refs_4_.refs_6_), custom_call_target="tpu_custom_call" | custom-call | flops 10000000 | bytes 843456 | tf_op jit(solution)/shard_map/volume/pallas_call | solution.py:29
  43.9 1.2 %injected.1 = (f32[4,8,16,128]{3,2,1,0:T(8,128)S(1)}, f32[4,4,16,128]{3,2,1,0:T(8,128)S(1)}, f32[4,4,16,128]{3,2,1,0:T(8,128)S(1)}, f32[4,8,8,128]{3,2,1,0:T(8,128)S(1)}, f32[4,8,8,128]{3,2,1,0:T(8,128)S(1)}) custom-call(f32[4,8,16,128]{3,2,1,0:T(8,128)S(1)} %copy-done.1, f32[3,8,16,128]{3,2,1,0:T(8,128)S(1)} %copy-done.3, f32[2,8,16,128]{3,2,1,0:T(8,128)S(1)} %copy-done.4, ...), custom_call_target="tpu_custom_call" | custom-call | flops 1000000 | bytes 3117536 | tf_op jit(solution)/shard_map/injected/pallas_call | solution.py:29
  46.1 0.7 collective-permute-start.15
  46.8 2.2 %collective-permute-start.14 = (f32[4,4,16,128]{3,2,1,0:T(8,128)S(1)}, f32[4,4,16,128]{3,2,1,0:T(8,128)S(1)}, u32[]{:S(2)}, u32[]{:S(2)}) collective-permute-start(f32[4,4,16,128]{3,2,1,0:T(8,128)S(1)} %get-tuple-element.60.refs_16_), channel_id=1, source_target_pairs={{0,4},{4,0},{8,12},{12,8},{16,20},{20,16},{24,28},{28,24},{1,5},{5... | collective-permute-start | bytes 393224 | tf_op jit(solution)/shard_map/ppermute | solution.py:48
  49.0 2.0 %flux.2.refs_7_.refs_0_ = f32[9,20,256]{2,1,0:T(8,128)S(1)} custom-call(f32[9,20,256]{2,1,0:T(8,128)S(1)} %volume.1.refs_19_.refs_0_, f32[9,16,1024]{2,1,0:T(8,128)S(1)} %get-tuple-element.50.refs_1_, f32[9,16,128]{2,1,0:T(8,128)S(1)} %get-tuple-element.51.refs_2_, f32[9,9,4,256]{3,2,1,0:T(4,128)S(1)} %bitcast.6, f32[10,4,20]{2,1,0:T(4,128)S(1)} %bitcast.14, ...), custom_call_target="tpu_custom_call" | custom-call | flops 20000000 | bytes 2641504 | tf_op jit(solution)/shard_map/flux/pallas_call | solution.py:29
  51.0 1.9 %collective-permute-done.14.refs_5_.refs_4_ = f32[4,4,16,128]{3,2,1,0:T(8,128)S(1)} collective-permute-done((f32[4,4,16,128]{3,2,1,0:T(8,128)S(1)}, f32[4,4,16,128]{3,2,1,0:T(8,128)S(1)}, u32[]{:S(2)}, u32[]{:S(2)}) %collective-permute-start.14) | collective-permute-done | bytes 131104 | tf_op jit(solution)/shard_map/ppermute | solution.py:48
  53.3 3.3 %collective-permute-start.16 = (f32[64,128]{1,0:T(8,128)S(1)}, f32[64,128]{1,0:T(8,128)S(1)}, u32[]{:S(2)}, u32[]{:S(2)}) collective-permute-start(f32[64,128]{1,0:T(8,128)S(1)} %get-tuple-element.67), channel_id=1, source_target_pairs={{0,1},{1,0},{2,3},{3,2},{4,5},{5,4},{6,7},{7,6},{8,9},{9,8},{10,11... | collective-permute-start | bytes 98312 | tf_op jit(solution)/shard_map/ppermute | solution.py:48
  58.0 5.7 %collective-permute-start.18 = (f32[64,128]{1,0:T(8,128)S(1)}, f32[64,128]{1,0:T(8,128)S(1)}, u32[]{:S(2)}, u32[]{:S(2)}) collective-permute-start(f32[64,128]{1,0:T(8,128)S(1)} %get-tuple-element.66.refs_6_), channel_id=1, source_target_pairs={{0,4},{4,0},{8,12},{12,8},{16,20},{20,16},{24,28},{28,24},{1,5},{5... | collective-permute-start | bytes 98312 | tf_op jit(solution)/shard_map/ppermute | solution.py:48
  64.2 1.4 %collective-permute-done.18.refs_6_ = f32[64,128]{1,0:T(8,128)S(1)} collective-permute-done((f32[64,128]{1,0:T(8,128)S(1)}, f32[64,128]{1,0:T(8,128)S(1)}, u32[]{:S(2)}, u32[]{:S(2)}) %collective-permute-start.18) | collective-permute-done | bytes 32800 | tf_op jit(solution)/shard_map/ppermute | solution.py:48
  65.8 2.1 %collective-permute-start.20 = (f32[4,8,8,128]{3,2,1,0:T(8,128)S(1)}, f32[4,8,8,128]{3,2,1,0:T(8,128)S(1)}, u32[]{:S(2)}, u32[]{:S(2)}) collective-permute-start(f32[4,8,8,128]{3,2,1,0:T(8,128)S(1)} %get-tuple-element.72), channel_id=1, source_target_pairs={{0,1},{1,0},{2,3},{3,2},{4,5},{5,4},{6,7},{7,6},{8,9},{9,8},{10,11... | collective-permute-start | bytes 393224 | tf_op jit(solution)/shard_map/ppermute | solution.py:48
  68.6 0.7 collective-permute-start.23
  69.3 5.6 %collective-permute-start.22 = (f32[4,4,16,128]{3,2,1,0:T(8,128)S(1)}, f32[4,4,16,128]{3,2,1,0:T(8,128)S(1)}, u32[]{:S(2)}, u32[]{:S(2)}) collective-permute-start(f32[4,4,16,128]{3,2,1,0:T(8,128)S(1)} %get-tuple-element.70.refs_16_), channel_id=1, source_target_pairs={{0,4},{4,0},{8,12},{12,8},{16,20},{20,16},{24,28},{28,24},{1,5},{5... | collective-permute-start | bytes 393224 | tf_op jit(solution)/shard_map/ppermute | solution.py:48
  74.9 2.7 %flux.3.refs_7_ = f32[9,20,256]{2,1,0:T(8,128)} custom-call(f32[9,20,256]{2,1,0:T(8,128)S(1)} %flux.2.refs_7_.refs_0_, f32[9,16,1024]{2,1,0:T(8,128)S(1)} %get-tuple-element.50.refs_1_, f32[9,16,128]{2,1,0:T(8,128)S(1)} %get-tuple-element.51.refs_2_, f32[9,9,4,256]{3,2,1,0:T(4,128)S(1)} %bitcast.7, f32[10,4,20]{2,1,0:T(4,128)S(1)} %bitcast.15, ...), custom_call_target="tpu_custom_call" | custom-call | flops 20000000 | bytes 2641504 | tf_op jit(solution)/shard_map/flux/pallas_call | solution.py:29
  77.6 2.5 %collective-permute-done.22.refs_5_.refs_4_ = f32[4,4,16,128]{3,2,1,0:T(8,128)S(1)} collective-permute-done((f32[4,4,16,128]{3,2,1,0:T(8,128)S(1)}, f32[4,4,16,128]{3,2,1,0:T(8,128)S(1)}, u32[]{:S(2)}, u32[]{:S(2)}) %collective-permute-start.22) | collective-permute-done | bytes 131104 | tf_op jit(solution)/shard_map/ppermute | solution.py:48
  80.1 0.9 %copy-done.7 = f32[9,20,256]{2,1,0:T(8,128)S(1)} copy-done((f32[9,20,256]{2,1,0:T(8,128)S(1)}, f32[9,20,256]{2,1,0:T(8,128)}, u32[]{:S(2)}) %copy-start.7) | copy-done | bytes 184344
  83.1 5.9 %collective-permute-start.26 = (f32[64,128]{1,0:T(8,128)S(1)}, f32[64,128]{1,0:T(8,128)S(1)}, u32[]{:S(2)}, u32[]{:S(2)}) collective-permute-start(f32[64,128]{1,0:T(8,128)S(1)} %get-tuple-element.76.refs_6_), channel_id=1, source_target_pairs={{0,4},{4,0},{8,12},{12,8},{16,20},{20,16},{24,28},{28,24},{1,5},{5... | collective-permute-start | bytes 98312 | tf_op jit(solution)/shard_map/ppermute | solution.py:48
  89.5 1.4 %collective-permute-done.26.refs_6_ = f32[64,128]{1,0:T(8,128)S(1)} collective-permute-done((f32[64,128]{1,0:T(8,128)S(1)}, f32[64,128]{1,0:T(8,128)S(1)}, u32[]{:S(2)}, u32[]{:S(2)}) %collective-permute-start.26) | collective-permute-done | bytes 32800 | tf_op jit(solution)/shard_map/ppermute | solution.py:48
  90.9 1.0 %velocity.3 = f32[4,8,16,128]{3,2,1,0:T(8,128)} custom-call(f32[4,8,16,128]{3,2,1,0:T(8,128)S(1)} %get-tuple-element.71.refs_0_, f32[1,8,16,128]{3,2,1,0:T(8,128)S(1)} %get-tuple-element.75.refs_1_, f32[2,8,16,128]{3,2,1,0:T(8,128)S(1)} %copy-done.4, f32[3,8,16,128]{3,2,1,0:T(8,128)S(1)} %advection.5.refs_3_, f32[64,128]{1,0:T(8,128)S(1)} %collective-permute-done.24.refs_4_, ...), custom_call_target="tpu_custom_call" | custom-call | flops 1000000 | bytes 1048576 | tf_op jit(solution)/shard_map/velocity/pallas_call | solution.py:29
  (71 shorter events, 10.5 us)
Async XLA Ops:
  2.6 14.2 %collective-permute-start.2 = (f32[8,4,16,128]{3,2,1,0:T(8,128)S(1)}, f32[8,4,16,128]{3,2,1,0:T(8,128)S(1)}, u32[]{:S(2)}, u32[]{:S(2)}) collective-permute-start(f32[8,4,16,128]{3,2,1,0:T(8,128)S(1)} %get-tuple-element.44), channel_id=1, source_target_pairs={{0,4},{4,0},{8,12},{12,8},{16,20},{20,16},{24,28},{28,24},{1,5},{5... | collective-permute-start | bytes 786440 | tf_op jit(solution)/shard_map/ppermute | solution.py:48
  5.6 11.2 %collective-permute-start.3 = (f32[8,4,16,128]{3,2,1,0:T(8,128)S(1)}, f32[8,4,16,128]{3,2,1,0:T(8,128)S(1)}, u32[]{:S(2)}, u32[]{:S(2)}) collective-permute-start(f32[8,4,16,128]{3,2,1,0:T(8,128)S(1)} %get-tuple-element.45), channel_id=1, source_target_pairs={{4,8},{8,4},{12,16},{16,12},{20,24},{24,20},{5,9},{9,5},{13,17},{1... | collective-permute-start | bytes 786440 | tf_op jit(solution)/shard_map/ppermute | solution.py:48
  6.3 7.3 %collective-permute-start = (f32[7,8,8,128]{3,2,1,0:T(8,128)S(1)}, f32[7,8,8,128]{3,2,1,0:T(8,128)S(1)}, u32[]{:S(2)}, u32[]{:S(2)}) collective-permute-start(f32[7,8,8,128]{3,2,1,0:T(8,128)S(1)} %get-tuple-element.42), channel_id=1, source_target_pairs={{0,1},{1,0},{2,3},{3,2},{4,5},{5,4},{6,7},{7,6},{8,9},{9,8},{10,11... | collective-permute-start | bytes 688136 | tf_op jit(solution)/shard_map/ppermute | solution.py:48
  6.4 7.3 %collective-permute-start.1 = (f32[7,8,8,128]{3,2,1,0:T(8,128)S(1)}, f32[7,8,8,128]{3,2,1,0:T(8,128)S(1)}, u32[]{:S(2)}, u32[]{:S(2)}) collective-permute-start(f32[7,8,8,128]{3,2,1,0:T(8,128)S(1)} %get-tuple-element.43), channel_id=1, source_target_pairs={{1,2},{2,1},{5,6},{6,5},{9,10},{10,9},{13,14},{14,13},{17,18},{18,... | collective-permute-start | bytes 688136 | tf_op jit(solution)/shard_map/ppermute | solution.py:48
  8.7 8.1 %copy-start.1 = (f32[4,8,16,128]{3,2,1,0:T(8,128)S(1)}, f32[4,8,16,128]{3,2,1,0:T(8,128)}, u32[]{:S(2)}) copy-start(f32[4,8,16,128]{3,2,1,0:T(8,128)} %refs_11_.3) | copy-start | bytes 786436
  8.7 8.1 %copy-start.3 = (f32[3,8,16,128]{3,2,1,0:T(8,128)S(1)}, f32[3,8,16,128]{3,2,1,0:T(8,128)}, u32[]{:S(2)}) copy-start(f32[3,8,16,128]{3,2,1,0:T(8,128)} %refs_1_.15) | copy-start | bytes 589828
  8.7 8.1 %copy-start.4 = (f32[2,8,16,128]{3,2,1,0:T(8,128)S(1)}, f32[2,8,16,128]{3,2,1,0:T(8,128)}, u32[]{:S(2)}) copy-start(f32[2,8,16,128]{3,2,1,0:T(8,128)} %refs_2_.13) | copy-start | bytes 393220
  17.2 3.6 %collective-permute-start.5 = (f32[168,128]{1,0:T(8,128)S(1)}, f32[168,128]{1,0:T(8,128)S(1)}, u32[]{:S(2)}, u32[]{:S(2)}) collective-permute-start(f32[168,128]{1,0:T(8,128)S(1)} %get-tuple-element.52), channel_id=1, source_target_pairs={{1,2},{2,1},{5,6},{6,5},{9,10},{10,9},{13,14},{14,13},{17,18},{18,... | collective-permute-start | bytes 258056 | tf_op jit(solution)/shard_map/ppermute | solution.py:48
  17.9 3.8 %collective-permute-start.4 = (f32[168,128]{1,0:T(8,128)S(1)}, f32[168,128]{1,0:T(8,128)S(1)}, u32[]{:S(2)}, u32[]{:S(2)}) collective-permute-start(f32[168,128]{1,0:T(8,128)S(1)} %get-tuple-element.49.refs_4_.refs_6_), channel_id=1, source_target_pairs={{0,1},{1,0},{2,3},{3,2},{4,5},{5,4},{6,7},{7,6},{8,9},{9,8},{10,11... | collective-permute-start | bytes 258056 | tf_op jit(solution)/shard_map/ppermute | solution.py:48
  21.8 22.1 %collective-permute-start.6 = (f32[168,128]{1,0:T(8,128)S(1)}, f32[168,128]{1,0:T(8,128)S(1)}, u32[]{:S(2)}, u32[]{:S(2)}) collective-permute-start(f32[168,128]{1,0:T(8,128)S(1)} %get-tuple-element.56), channel_id=1, source_target_pairs={{0,4},{4,0},{8,12},{12,8},{16,20},{20,16},{24,28},{28,24},{1,5},{5... | collective-permute-start | bytes 258056 | tf_op jit(solution)/shard_map/ppermute | solution.py:48
  24.9 19.0 %collective-permute-start.7 = (f32[168,128]{1,0:T(8,128)S(1)}, f32[168,128]{1,0:T(8,128)S(1)}, u32[]{:S(2)}, u32[]{:S(2)}) collective-permute-start(f32[168,128]{1,0:T(8,128)S(1)} %get-tuple-element.57), channel_id=1, source_target_pairs={{4,8},{8,4},{12,16},{16,12},{20,24},{24,20},{5,9},{9,5},{13,17},{1... | collective-permute-start | bytes 258056 | tf_op jit(solution)/shard_map/ppermute | solution.py:48
  25.5 18.3 %collective-permute-start.9 = (f32[136,128]{1,0:T(8,128)S(1)}, f32[136,128]{1,0:T(8,128)S(1)}, u32[]{:S(2)}, u32[]{:S(2)}) collective-permute-start(f32[136,128]{1,0:T(8,128)S(1)} %get-tuple-element.58), channel_id=1, source_target_pairs={{8,16},{16,8},{12,20},{20,12},{9,17},{17,9},{13,21},{21,13},{10,18... | collective-permute-start | bytes 208904 | tf_op jit(solution)/shard_map/ppermute | solution.py:48
  26.2 17.7 %collective-permute-start.8 = (f32[136,128]{1,0:T(8,128)S(1)}, f32[136,128]{1,0:T(8,128)S(1)}, u32[]{:S(2)}, u32[]{:S(2)}) collective-permute-start(f32[136,128]{1,0:T(8,128)S(1)} %get-tuple-element.58), channel_id=1, source_target_pairs={{0,8},{8,0},{4,12},{12,4},{16,24},{24,16},{20,28},{28,20},{1,9},{9... | collective-permute-start | bytes 208904 | tf_op jit(solution)/shard_map/ppermute | solution.py:48
  31.9 0.7 collective-permute-start.11
  32.6 11.3 %collective-permute-start.10 = (f32[8,128]{1,0:T(8,128)S(1)}, f32[8,128]{1,0:T(8,128)S(1)}, u32[]{:S(2)}, u32[]{:S(2)}) collective-permute-start(f32[8,128]{1,0:T(8,128)S(1)} %get-tuple-element.59.refs_13_), channel_id=1, source_target_pairs={{0,12},{12,0},{4,16},{16,4},{8,20},{20,8},{1,13},{13,1},{5,17},{17... | collective-permute-start | bytes 12296 | tf_op jit(solution)/shard_map/ppermute | solution.py:48
  43.8 5.2 %copy-start.5 = (f32[4,9,9,256]{3,0,2,1:T(4,128)S(1)}, f32[4,9,9,256]{3,0,2,1:T(4,128)}, u32[]{:S(2)}) copy-start(f32[4,9,9,256]{3,0,2,1:T(4,128)} %param.15) | copy-start | bytes 995332
  45.1 5.8 %collective-permute-start.12 = (f32[4,8,8,128]{3,2,1,0:T(8,128)S(1)}, f32[4,8,8,128]{3,2,1,0:T(8,128)S(1)}, u32[]{:S(2)}, u32[]{:S(2)}) collective-permute-start(f32[4,8,8,128]{3,2,1,0:T(8,128)S(1)} %get-tuple-element.62), channel_id=1, source_target_pairs={{0,1},{1,0},{2,3},{3,2},{4,5},{5,4},{6,7},{7,6},{8,9},{9,8},{10,11... | collective-permute-start | bytes 393224 | tf_op jit(solution)/shard_map/ppermute | solution.py:48
  45.5 5.5 %collective-permute-start.13 = (f32[4,8,8,128]{3,2,1,0:T(8,128)S(1)}, f32[4,8,8,128]{3,2,1,0:T(8,128)S(1)}, u32[]{:S(2)}, u32[]{:S(2)}) collective-permute-start(f32[4,8,8,128]{3,2,1,0:T(8,128)S(1)} %get-tuple-element.63), channel_id=1, source_target_pairs={{1,2},{2,1},{5,6},{6,5},{9,10},{10,9},{13,14},{14,13},{17,18},{18,... | collective-permute-start | bytes 393224 | tf_op jit(solution)/shard_map/ppermute | solution.py:48
  46.1 4.8 %collective-permute-start.15 = (f32[4,4,16,128]{3,2,1,0:T(8,128)S(1)}, f32[4,4,16,128]{3,2,1,0:T(8,128)S(1)}, u32[]{:S(2)}, u32[]{:S(2)}) collective-permute-start(f32[4,4,16,128]{3,2,1,0:T(8,128)S(1)} %get-tuple-element.64), channel_id=1, source_target_pairs={{4,8},{8,4},{12,16},{16,12},{20,24},{24,20},{5,9},{9,5},{13,17},{1... | collective-permute-start | bytes 393224 | tf_op jit(solution)/shard_map/ppermute | solution.py:48
  46.8 6.1 %collective-permute-start.14 = (f32[4,4,16,128]{3,2,1,0:T(8,128)S(1)}, f32[4,4,16,128]{3,2,1,0:T(8,128)S(1)}, u32[]{:S(2)}, u32[]{:S(2)}) collective-permute-start(f32[4,4,16,128]{3,2,1,0:T(8,128)S(1)} %get-tuple-element.60.refs_16_), channel_id=1, source_target_pairs={{0,4},{4,0},{8,12},{12,8},{16,20},{20,16},{24,28},{28,24},{1,5},{5... | collective-permute-start | bytes 393224 | tf_op jit(solution)/shard_map/ppermute | solution.py:48
  53.3 10.8 %collective-permute-start.16 = (f32[64,128]{1,0:T(8,128)S(1)}, f32[64,128]{1,0:T(8,128)S(1)}, u32[]{:S(2)}, u32[]{:S(2)}) collective-permute-start(f32[64,128]{1,0:T(8,128)S(1)} %get-tuple-element.67), channel_id=1, source_target_pairs={{0,1},{1,0},{2,3},{3,2},{4,5},{5,4},{6,7},{7,6},{8,9},{9,8},{10,11... | collective-permute-start | bytes 98312 | tf_op jit(solution)/shard_map/ppermute | solution.py:48
  56.6 7.5 %collective-permute-start.17 = (f32[64,128]{1,0:T(8,128)S(1)}, f32[64,128]{1,0:T(8,128)S(1)}, u32[]{:S(2)}, u32[]{:S(2)}) collective-permute-start(f32[64,128]{1,0:T(8,128)S(1)} %get-tuple-element.68), channel_id=1, source_target_pairs={{1,2},{2,1},{5,6},{6,5},{9,10},{10,9},{13,14},{14,13},{17,18},{18,... | collective-permute-start | bytes 98312 | tf_op jit(solution)/shard_map/ppermute | solution.py:48
  57.3 6.9 %collective-permute-start.19 = (f32[64,128]{1,0:T(8,128)S(1)}, f32[64,128]{1,0:T(8,128)S(1)}, u32[]{:S(2)}, u32[]{:S(2)}) collective-permute-start(f32[64,128]{1,0:T(8,128)S(1)} %get-tuple-element.69), channel_id=1, source_target_pairs={{4,8},{8,4},{12,16},{16,12},{20,24},{24,20},{5,9},{9,5},{13,17},{1... | collective-permute-start | bytes 98312 | tf_op jit(solution)/shard_map/ppermute | solution.py:48
  58.0 7.6 %collective-permute-start.18 = (f32[64,128]{1,0:T(8,128)S(1)}, f32[64,128]{1,0:T(8,128)S(1)}, u32[]{:S(2)}, u32[]{:S(2)}) collective-permute-start(f32[64,128]{1,0:T(8,128)S(1)} %get-tuple-element.66.refs_6_), channel_id=1, source_target_pairs={{0,4},{4,0},{8,12},{12,8},{16,20},{20,16},{24,28},{28,24},{1,5},{5... | collective-permute-start | bytes 98312 | tf_op jit(solution)/shard_map/ppermute | solution.py:48
  65.8 11.8 %collective-permute-start.20 = (f32[4,8,8,128]{3,2,1,0:T(8,128)S(1)}, f32[4,8,8,128]{3,2,1,0:T(8,128)S(1)}, u32[]{:S(2)}, u32[]{:S(2)}) collective-permute-start(f32[4,8,8,128]{3,2,1,0:T(8,128)S(1)} %get-tuple-element.72), channel_id=1, source_target_pairs={{0,1},{1,0},{2,3},{3,2},{4,5},{5,4},{6,7},{7,6},{8,9},{9,8},{10,11... | collective-permute-start | bytes 393224 | tf_op jit(solution)/shard_map/ppermute | solution.py:48
  68.0 9.6 %collective-permute-start.21 = (f32[4,8,8,128]{3,2,1,0:T(8,128)S(1)}, f32[4,8,8,128]{3,2,1,0:T(8,128)S(1)}, u32[]{:S(2)}, u32[]{:S(2)}) collective-permute-start(f32[4,8,8,128]{3,2,1,0:T(8,128)S(1)} %get-tuple-element.73), channel_id=1, source_target_pairs={{1,2},{2,1},{5,6},{6,5},{9,10},{10,9},{13,14},{14,13},{17,18},{18,... | collective-permute-start | bytes 393224 | tf_op jit(solution)/shard_map/ppermute | solution.py:48
  68.6 9.0 %collective-permute-start.23 = (f32[4,4,16,128]{3,2,1,0:T(8,128)S(1)}, f32[4,4,16,128]{3,2,1,0:T(8,128)S(1)}, u32[]{:S(2)}, u32[]{:S(2)}) collective-permute-start(f32[4,4,16,128]{3,2,1,0:T(8,128)S(1)} %get-tuple-element.74), channel_id=1, source_target_pairs={{4,8},{8,4},{12,16},{16,12},{20,24},{24,20},{5,9},{9,5},{13,17},{1... | collective-permute-start | bytes 393224 | tf_op jit(solution)/shard_map/ppermute | solution.py:48
  69.3 10.8 %collective-permute-start.22 = (f32[4,4,16,128]{3,2,1,0:T(8,128)S(1)}, f32[4,4,16,128]{3,2,1,0:T(8,128)S(1)}, u32[]{:S(2)}, u32[]{:S(2)}) collective-permute-start(f32[4,4,16,128]{3,2,1,0:T(8,128)S(1)} %get-tuple-element.70.refs_16_), channel_id=1, source_target_pairs={{0,4},{4,0},{8,12},{12,8},{16,20},{20,16},{24,28},{28,24},{1,5},{5... | collective-permute-start | bytes 393224 | tf_op jit(solution)/shard_map/ppermute | solution.py:48
  81.4 8.1 %collective-permute-start.24 = (f32[64,128]{1,0:T(8,128)S(1)}, f32[64,128]{1,0:T(8,128)S(1)}, u32[]{:S(2)}, u32[]{:S(2)}) collective-permute-start(f32[64,128]{1,0:T(8,128)S(1)} %get-tuple-element.77), channel_id=1, source_target_pairs={{0,1},{1,0},{2,3},{3,2},{4,5},{5,4},{6,7},{7,6},{8,9},{9,8},{10,11... | collective-permute-start | bytes 98312 | tf_op jit(solution)/shard_map/ppermute | solution.py:48
  81.8 7.7 %collective-permute-start.25 = (f32[64,128]{1,0:T(8,128)S(1)}, f32[64,128]{1,0:T(8,128)S(1)}, u32[]{:S(2)}, u32[]{:S(2)}) collective-permute-start(f32[64,128]{1,0:T(8,128)S(1)} %get-tuple-element.78), channel_id=1, source_target_pairs={{1,2},{2,1},{5,6},{6,5},{9,10},{10,9},{13,14},{14,13},{17,18},{18,... | collective-permute-start | bytes 98312 | tf_op jit(solution)/shard_map/ppermute | solution.py:48
  82.4 7.1 %collective-permute-start.27 = (f32[64,128]{1,0:T(8,128)S(1)}, f32[64,128]{1,0:T(8,128)S(1)}, u32[]{:S(2)}, u32[]{:S(2)}) collective-permute-start(f32[64,128]{1,0:T(8,128)S(1)} %get-tuple-element.79), channel_id=1, source_target_pairs={{4,8},{8,4},{12,16},{16,12},{20,24},{24,20},{5,9},{9,5},{13,17},{1... | collective-permute-start | bytes 98312 | tf_op jit(solution)/shard_map/ppermute | solution.py:48
  83.1 7.7 %collective-permute-start.26 = (f32[64,128]{1,0:T(8,128)S(1)}, f32[64,128]{1,0:T(8,128)S(1)}, u32[]{:S(2)}, u32[]{:S(2)}) collective-permute-start(f32[64,128]{1,0:T(8,128)S(1)} %get-tuple-element.76.refs_6_), channel_id=1, source_target_pairs={{0,4},{4,0},{8,12},{12,8},{16,20},{20,16},{24,28},{28,24},{1,5},{5... | collective-permute-start | bytes 98312 | tf_op jit(solution)/shard_map/ppermute | solution.py:48
  (12 other events, 34.6 us)
